TPU v7x, 256 devices: a whole 4x4x8 slice. The times are simulated.
256 devices in a mesh: dp: 32 (over x, y, z_hi), feat: 8 (over z_lo, core).
Axes of the slice: x: 4, y: 4, z: 8 (z_hi: 2, z_lo: 4; z = z_hi * 4 + z_lo), core: 2. Of those that a mesh axis runs over, the one named last changes fastest.
Arguments:
- embeds: bfloat16 [512, 2048, 128], P('dp', 'feat'), may hold values from -6 to 6
- proj_weight: bfloat16 [2048, 256], P('feat'), may hold values from -0.01171875 to 0.01171875
- hidden_weight: bfloat16 [256, 512], replicated, may hold values from -0.375 to 0.375
- out_weight: bfloat16 [512, 128], replicated, may hold values from -0.25 to 0.25
- cotangent: bfloat16 [512, 2048, 128], P('dp', 'feat'), may hold values from -3 to 3
Outputs:
- embed_grad: bfloat16 [512, 2048, 128], P('dp', 'feat')
- proj_grad: float32 [2048, 256], P('feat', 'dp')
- hidden_grad: float32 [256, 512], P('dp')
- out_grad: float32 [512, 128], P('dp')
All inputs are finite; a program needn't handle non-finite values.
Results may differ from a plain program's by a relative error of at most 0.025.
Values may be sent and summed in bfloat16 or wider, within the bound.
A program may use at most 64 MiB of HBM per device.

v0:
```python
import math

import jax
import jax.numpy as jnp
from jax import lax
from jax.sharding import PartitionSpec as P


def local(embeds, proj_weight, hidden_weight, out_weight, cotangent):
    samples, group, width = embeds.shape
    rank = proj_weight.shape[1]
    hidden_width = hidden_weight.shape[1]
    dp_count = lax.axis_size("dp")
    mlp_scale = 4.0 / (samples * dp_count)
    proj_scale = 1.0 / (samples * dp_count * math.sqrt(width))
    mixer_part = jnp.einsum("bfd,fk->bdk", embeds, proj_weight, preferred_element_type=jnp.float32)
    mixer = lax.psum(mixer_part.astype(jnp.bfloat16), "feat")
    inter = jnp.einsum("bfd,bdk->bfk", embeds, mixer, preferred_element_type=jnp.float32).astype(
        jnp.bfloat16
    )
    flat_inter = inter.reshape(-1, rank)
    pre = jnp.dot(flat_inter, hidden_weight, preferred_element_type=jnp.float32)
    sig = jax.nn.sigmoid(pre)
    act = (pre * sig).astype(jnp.bfloat16)
    flat_cot = cotangent.reshape(-1, width)
    act_cot = jnp.einsum("rd,hd->rh", flat_cot, out_weight, preferred_element_type=jnp.float32)
    pre_cot = (act_cot * sig * (1.0 + pre * (1.0 - sig))).astype(jnp.bfloat16)
    out_term = jnp.einsum("rh,rd->hd", act, flat_cot, preferred_element_type=jnp.float32)
    hidden_term = jnp.einsum("rk,rh->kh", flat_inter, pre_cot, preferred_element_type=jnp.float32)
    inter_cot = jnp.einsum("rh,kh->rk", pre_cot, hidden_weight, preferred_element_type=jnp.float32)
    inter_cot = inter_cot.astype(jnp.bfloat16).reshape(samples, group, rank)
    cot_part = jnp.einsum("bfd,bfk->bdk", embeds, inter_cot, preferred_element_type=jnp.float32)
    mixer_cot = lax.psum(cot_part.astype(jnp.bfloat16), "feat")
    grad = (
        cotangent.astype(jnp.float32)
        + jnp.einsum("bfk,bdk->bfd", inter_cot, mixer, preferred_element_type=jnp.float32)
        + jnp.einsum("fk,bdk->bfd", proj_weight, mixer_cot, preferred_element_type=jnp.float32)
    )
    embed_grad = grad.astype(jnp.bfloat16)
    proj_term = jnp.einsum("bfd,bdk->fk", embeds, mixer_cot, preferred_element_type=jnp.float32)
    hidden_sum, out_sum = lax.psum((hidden_term, out_term), ("dp", "feat"))
    proj_sum = lax.psum(proj_term, "dp")
    position = lax.axis_index("dp")
    hidden_rows = rank // dp_count
    out_rows = hidden_width // dp_count
    hidden_grad = lax.dynamic_slice_in_dim(hidden_sum, position * hidden_rows, hidden_rows, 0)
    out_grad = lax.dynamic_slice_in_dim(out_sum, position * out_rows, out_rows, 0)
    proj_grad = lax.dynamic_slice_in_dim(proj_sum, position * hidden_rows, hidden_rows, 1)
    return (embed_grad, proj_grad * proj_scale, hidden_grad * mlp_scale, out_grad * mlp_scale)


def solution(mesh):
    placed = (P("dp", "feat", None), P("feat", None), P(), P(), P("dp", "feat", None))
    return jax.shard_map(
        local,
        mesh=mesh,
        in_specs=placed,
        out_specs=(P("dp", "feat", None), P("feat", "dp"), P("dp", None), P("dp", None)),
        check_vma=False,
    )
```

profile of v0, /device:TPU:32, one launch (start us, length us, event | category | flops | bytes accessed | tf_op | source)
XLA Modules:
  0.0 863.3 jit_solution(3742269911456863472)
XLA Ops:
  7.2 0.0 all-reduce.6.cloned.1.call-start
  7.2 1.2 copy-done
  8.4 2.4 convolution_convert_fusion.3
  10.8 0.0 all-reduce.12.cloned.1.call-start
  10.8 74.3 %all-reduce.6.cloned.1.call-done = bf16[16,128,256]{2,1,0:T(8,128)(2,1)} async-done(((bf16[16,128,256]{2,1,0:T(8,128)(2,1)}), bf16[16,128,256]{2,1,0:T(8,128)(2,1)}) %all-reduce.6.cloned.1.call-update) | async-done | bytes 1048592 | tf_op jit(solution)/shard_map/psum | solution.py:17
  85.1 1.9 convolution_convert_fusion.1
  87.1 1.2 fusion.6
  88.4 3.3 fusion
  91.6 3.4 multiply_convert_fusion.1
  95.1 1.9 copy-done.5
  97.0 2.0 fusion.8
  99.1 0.0 all-reduce.8.cloned.1.call-start
  99.1 3.5 convolution_convert_fusion
  102.6 1.7 fusion.2
  104.4 0.0 all-reduce.10.cloned.1.call-start
  104.4 3.3 fusion.7
  107.7 245.5 %all-reduce.12.cloned.1.call-done = (f32[256,512]{1,0:T(8,128)}, f32[512,128]{1,0:T(8,128)}) async-done(((f32[256,512]{1,0:T(8,128)}, f32[512,128]{1,0:T(8,128)}), (f32[256,512]{1,0:T(8,128)}, f32[512,128]{1,0:T(8,128)})) %all-reduce.12.cloned.1.call-update) | async-done | bytes 786448 | tf_op jit(solution)/shard_map/psum | solution.py:41
  353.2 1.3 dynamic-slice_multiply_fusion.1
  354.5 1.3 dynamic-slice_multiply_fusion
  355.8 73.0 %all-reduce.8.cloned.1.call-done = bf16[16,128,256]{1,2,0:T(8,128)(2,1)} async-done(((bf16[16,128,256]{1,2,0:T(8,128)(2,1)}), bf16[16,128,256]{1,2,0:T(8,128)(2,1)}) %all-reduce.8.cloned.1.call-update) | async-done | bytes 1048592 | tf_op jit(solution)/shard_map/psum | solution.py:33
  428.9 2.4 convolution_bitcast_fusion
  431.3 3.6 fusion.1
  434.9 420.6 %all-reduce.10.cloned.1.call-done = f32[256,256]{0,1:T(8,128)} async-done(((f32[256,256]{0,1:T(8,128)}), f32[256,256]{0,1:T(8,128)}) %all-reduce.10.cloned.1.call-update) | async-done | bytes 262160 | tf_op jit(solution)/shard_map/psum | solution.py:42
  855.5 1.3 dynamic-slice_multiply_fusion.2
  (14 shorter events, 0.1 us)
Async XLA Ops:
  7.2 1.2 copy-start
  7.2 79.9 %copy-start.3 = (bf16[256,512]{1,0:T(8,128)(2,1)S(1)}, bf16[256,512]{1,0:T(8,128)(2,1)}, u32[]{:S(2)}) copy-start(bf16[256,512]{1,0:T(8,128)(2,1)} %param.7) | copy-start | bytes 786436
  7.2 77.9 %all-reduce.6.cloned.1.call-start = ((), (), s32[]{:S(2)}) async-start(), calls=%async_computation | async-start | bytes 2097152 | tf_op jit(solution)/shard_map/psum | solution.py:17
  10.8 342.4 %all-reduce.12.cloned.1.call-start = ((), (), s32[]{:S(2)}) async-start(), calls=%async_computation.3 | async-start | bytes 1572864 | tf_op jit(solution)/shard_map/psum | solution.py:41
  87.1 1.3 copy-start.1
  88.3 3.3 copy-start.4
  95.1 1.9 copy-start.5
  99.1 329.8 %all-reduce.8.cloned.1.call-start = ((), (), s32[]{:S(2)}) async-start(), calls=%async_computation.1 | async-start | bytes 2097152 | tf_op jit(solution)/shard_map/psum | solution.py:33
  104.4 326.9 %copy-start.2 = (bf16[256,256]{1,0:T(8,128)(2,1)S(1)}, bf16[256,256]{1,0:T(8,128)(2,1)}, u32[]{:S(2)}) copy-start(bf16[256,256]{1,0:T(8,128)(2,1)} %param.6) | copy-start | bytes 393220
  104.4 751.1 %all-reduce.10.cloned.1.call-start = ((), (), s32[]{:S(2)}) async-start(), calls=%async_computation.2 | async-start | bytes 524288 | tf_op jit(solution)/shard_map/psum | solution.py:42
Sparse Core Ops, SparseCore 0:
  11.2 73.8 all-reduce.5
  99.2 253.9 all-reduce.11
  356.6 72.1 all-reduce.7
  431.5 423.9 all-reduce.9
where the time goes:
time: 864 us; the launch traced here: 863 us
  waiting for transfers between devices  814 us (94%)
  matrix products  28.8 us (3%)
  between operations  13.9 us (2%)
    psum x1, waiting for transfers between devices, local(): proj_sum = lax.psum(proj_term, 'dp')  421 us
    psum x1, waiting for transfers between devices, local(): hidden_sum, out_sum = lax.psum((hidden_term, out_term), ('dp', 'feat'))  245 us
    psum x1, waiting for transfers between devices, local(): mixer = lax.psum(mixer_part.astype(jnp.bfloat16), 'feat')  74.3 us
    psum x1, waiting for transfers between devices, local(): mixer_cot = lax.psum(cot_part.astype(jnp.bfloat16), 'feat')  73 us
  transfers between devices with their start and end apart: 4, of which 4 were waited for; matrix products, arithmetic and copies ran while one was open for 2% of the time, Pallas kernels for 0%

commit v1 on v0

v1 whole, which is shorter than its diff:
```python
import functools
import math

import jax
import jax.numpy as jnp
from jax import lax
from jax.experimental import pallas as pl
from jax.experimental.pallas import tpu as pltpu
from jax.sharding import PartitionSpec as P

MESH = pl.DeviceIdType.MESH
BF = jnp.bfloat16
F32 = jnp.float32

LAG_TOTAL = 4
LAG_SHARE = 8
LAG_MLP = 10
LAG2_FIRST = 12
LAG2_PAIR = 16
LAG2_TOTAL = 20
LAG2_SHARE = 24
LAG2_FINAL = 26


def nn(a, b):
    return lax.dot_general(a, b, (((1,), (0,)), ((), ())), preferred_element_type=F32)


def nt(a, b):
    return lax.dot_general(a, b, (((1,), (1,)), ((), ())), preferred_element_type=F32)


def tn(a, b):
    return lax.dot_general(a, b, (((0,), (0,)), ((), ())), preferred_element_type=F32)


def kernel(
    samples, e_hbm, p_hbm, w1_hbm, w2_hbm, c_hbm,
    eg_hbm, pg_ref, hg_ref, og_ref,
    e_ref, p_ref, w1_ref, w2_ref, c_ref, pt_ref, w1t_ref, w2h_ref,
    part, land_a, chip, land_b, pair, land_c, full,
    gacc, stage, hid_acc, out_acc, proj_acc,
    w_mine, w_buddy, w_chip, w_x, w_xs, w_y, w_ys, w_h, w_hs, w_z,
    p_mine, p_x, p_xs, p_y, p_ys, p_h,
    load_sem, store_sem, ssem, rsem, wss, wrs, pss, prs,
):
    dp, ft = lax.axis_index("dp"), lax.axis_index("feat")
    x, y, hi = dp // 8, (dp // 2) % 4, dp % 2
    z, c = ft // 2, ft % 2
    hub = (z == 1) | (z == 2)
    outer = (z == 0) | (z == 3)
    half = (c + z) % 2
    mine = pl.ds(pl.multiple_of(half * 128, 128), 128)
    other = pl.ds(pl.multiple_of((1 - half) * 128, 128), 128)
    buddy = (dp, z * 2 + 1 - c)
    edge_z = jnp.where(z == 0, 1, jnp.where(z == 1, 0, jnp.where(z == 2, 3, 2)))
    edge = (dp, edge_z * 2 + 1 - c)
    across = (dp, (3 - z) * 2 + 1 - c)
    far = (x * 8 + y * 2 + 1 - hi, ft)
    xs = [(((x + d) % 4) * 8 + y * 2 + hi, ft) for d in (1, 2, 3)]
    ys = [(x * 8 + ((y + d) % 4) * 2 + hi, ft) for d in (1, 2, 3)]
    feats = [(dp, (ft + d) % 8) for d in range(1, 8)]

    barrier = pltpu.get_barrier_semaphore()
    peers = feats + xs + ys + [far]
    for peer in peers:
        pl.semaphore_signal(barrier, inc=1, device_id=peer, device_id_type=MESH)

    loads = [
        pltpu.make_async_copy(src, dst, load_sem.at[i])
        for i, (src, dst) in enumerate(
            ((p_hbm, p_ref), (e_hbm, e_ref), (w1_hbm, w1_ref), (w2_hbm, w2_ref), (c_hbm, c_ref))
        )
    ]
    for load in loads:
        load.start()

    def send(src, dst, s_sem, r_sem, device):
        return pltpu.make_async_remote_copy(
            src_ref=src, dst_ref=dst, send_sem=s_sem, recv_sem=r_sem,
            device_id=device, device_id_type=MESH,
        )

    def to_buddy(q, s):
        return send(part.at[q, s, other], land_a.at[q, s], ssem.at[q, 0], rsem.at[q, s, 0], buddy)

    def to_hub(q, s):
        return send(chip.at[q, s], land_b.at[q, s], ssem.at[q, 1], rsem.at[q, s, 1], edge)

    def to_across(q, s):
        return send(pair.at[q, s], land_c.at[q, s], ssem.at[q, 1], rsem.at[q, s, 2], across)

    def to_outer(q, s):
        ref = full.at[q, s, mine]
        return send(ref, ref, ssem.at[q, 2], rsem.at[q, s, 1], edge)

    def share(q, s):
        ref = full.at[q, s, mine]
        return send(ref, ref, ssem.at[q, 3], rsem.at[q, s, 3], buddy)

    def first(q, s):
        to_buddy(q, s).wait_recv()
        chip[q, s] = (part[q, s, mine].astype(F32) + land_a[q, s].astype(F32)).astype(BF)
        to_hub(q, s).start()

    def paired(q, s):
        to_buddy(q, s).wait_recv()
        to_hub(q, s).wait_recv()
        total = part[q, s, mine].astype(F32) + land_a[q, s].astype(F32) + land_b[q, s].astype(F32)
        pair[q, s] = total.astype(BF)
        to_across(q, s).start()

    def totalled(q, s):
        to_across(q, s).wait_recv()
        full[q, s, mine] = (pair[q, s].astype(F32) + land_c[q, s].astype(F32)).astype(BF)
        to_outer(q, s).start()
        share(q, s).start()

    def shared(q, s):
        to_outer(q, s).wait_recv()
        share(q, s).start()

    loads[0].wait()
    pt_ref[...] = p_ref[...].T
    loads[1].wait()
    pl.semaphore_wait(barrier, len(peers))

    def start_sample(s, carry):
        part[0, s] = nn(pt_ref[...], e_ref[s]).astype(BF)
        to_buddy(0, s).start()
        return carry

    lax.fori_loop(0, samples, start_sample, 0)

    @pl.when(outer)
    def _():
        def body(s, carry):
            first(0, s)
            return carry

        lax.fori_loop(0, samples, body, 0)

    hid_acc[...] = jnp.zeros_like(hid_acc)
    out_acc[...] = jnp.zeros_like(out_acc)
    proj_acc[...] = jnp.zeros_like(proj_acc)
    for load in loads[2:]:
        load.wait()
    w1t_ref[...] = (w1_ref[...].T.astype(F32) * 0.5).astype(BF)
    w2h_ref[...] = (w2_ref[...].astype(F32) * 0.5).astype(BF)

    def mlp(s):
        share(0, s).wait_recv()
        emb, cot, mix = e_ref[s], c_ref[s], full[0, s]
        inter = nt(mix, emb).astype(BF)
        u = nn(w1t_ref[...], inter)
        act_cot = nt(w2h_ref[...], cot)
        t = jnp.tanh(u)
        p = 1.0 + t
        a = u * p
        pre_cot = (act_cot * (p + a * (1.0 - t))).astype(BF)
        out_acc[...] += nn(a.astype(BF), cot)
        hid_acc[...] += nt(inter, pre_cot)
        inter_cot = nn(w1_ref[...], pre_cot).astype(BF)
        part[1, s] = nn(inter_cot, emb).astype(BF)
        to_buddy(1, s).start()
        gacc[s] = cot.astype(F32) + tn(inter_cot, mix)

    def final(s):
        share(1, s).wait_recv()
        mix_cot = full[1, s]
        stage[s] = (gacc[s] + nn(p_ref[...], mix_cot)).astype(BF)
        pltpu.make_async_copy(stage.at[s], eg_hbm.at[s], store_sem).start()
        proj_acc[...] += nt(mix_cot, e_ref[s])

    w_core = send(w_mine.at[:, 1 - c], w_buddy, wss.at[0], wrs.at[0], buddy)
    w_xc = [
        send(w_chip.at[pl.ds(((x + d) % 4) * 4, 4)], w_x.at[d - 1], wss.at[d], wrs.at[d], xs[d - 1])
        for d in (1, 2, 3)
    ]
    w_yc = [
        send(w_xs.at[(y + d) % 4], w_y.at[d - 1], wss.at[3 + d], wrs.at[3 + d], ys[d - 1])
        for d in (1, 2, 3)
    ]
    w_hc = send(w_ys, w_h, wss.at[7], wrs.at[7], far)
    w_zc = [
        send(w_hs, w_z.at[z], wss.at[8 + i], wrs.at[8 + z], feats[i]) for i in range(7)
    ]

    def w_first():
        hid = hid_acc[...].reshape(16, 2, 8, 512)
        hid = jnp.concatenate([hid[..., :256], hid[..., 256:]], axis=2)
        w_mine[..., :256] = hid.astype(BF)
        w_mine[..., 256:] = out_acc[...].reshape(16, 2, 16, 128).astype(BF)
        w_core.start()

    def w_along_x():
        w_core.wait_recv()
        w_chip[...] = (w_mine[:, c].astype(F32) + w_buddy[...].astype(F32)).astype(BF)
        for copy in w_xc:
            copy.start()

    def w_along_y():
        total = w_chip[pl.ds(x * 4, 4)].astype(F32)
        for d in range(3):
            w_xc[d].wait_recv()
            total += w_x[d].astype(F32)
        w_xs[...] = total.astype(BF)
        for copy in w_yc:
            copy.start()

    def w_along_z():
        total = w_xs[y].astype(F32)
        for d in range(3):
            w_yc[d].wait_recv()
            total += w_y[d].astype(F32)
        w_ys[...] = total.astype(BF)

        @pl.when(c != hi)
        def _():
            w_hc.start()

    def w_along_feat():
        @pl.when(c == hi)
        def _():
            w_hc.wait_recv()
            total = (w_ys[...].astype(F32) + w_h[...].astype(F32)).astype(BF)
            w_hs[...] = total
            w_z[z] = total
            for copy in w_zc:
                copy.start()

    def w_last():
        total = jnp.zeros((16, 384), F32)
        for source in range(4):
            @pl.when((z != source) | (c != hi))
            def _():
                send(w_hs, w_z.at[source], wss.at[8], wrs.at[8 + source], buddy).wait_recv()

        for source in range(4):
            total += w_z[source].astype(F32)
        hg_ref[:, :256] = total[:8, :256]
        hg_ref[:, 256:] = total[8:, :256]
        og_ref[...] = total[:, 256:]

    def during(t, start, stop, act):
        @pl.when((t >= start) & (t < stop))
        def _():
            act()

    def step(t, carry):
        def on(lag, who, act):
            @pl.when((t >= lag) & (t < lag + samples) & who)
            def _():
                act(t - lag)

        def once(at, act):
            @pl.when(t == at)
            def _():
                act()

        everyone = t >= 0
        on(0, hub, lambda s: paired(0, s))
        on(LAG_TOTAL, hub, lambda s: totalled(0, s))
        on(LAG_SHARE, outer, lambda s: shared(0, s))
        on(LAG2_FIRST, outer, lambda s: first(1, s))
        on(LAG2_PAIR, hub, lambda s: paired(1, s))
        on(LAG2_TOTAL, hub, lambda s: totalled(1, s))
        on(LAG2_SHARE, outer, lambda s: shared(1, s))
        on(LAG_MLP, everyone, mlp)
        once(samples + LAG_MLP, w_first)
        once(samples + LAG_MLP + 2, w_along_x)
        once(samples + LAG_MLP + 7, w_along_y)
        once(samples + LAG_MLP + 12, w_along_z)
        on(LAG2_FINAL, everyone, final)
        return carry

    lax.fori_loop(0, samples + LAG2_FINAL, step, 0)

    p_xc = [
        send(p_mine.at[pl.ds(((x + d) % 4) * 4, 4)], p_x.at[d - 1], pss.at[d], prs.at[d], xs[d - 1])
        for d in (1, 2, 3)
    ]
    p_yc = [
        send(p_xs.at[(y + d) % 4], p_y.at[d - 1], pss.at[3 + d], prs.at[3 + d], ys[d - 1])
        for d in (1, 2, 3)
    ]
    p_hc = send(p_ys.at[1 - hi], p_h, pss.at[0], prs.at[0], far)
    proj = proj_acc[...].reshape(16, 2, 8, 256)
    proj = jnp.concatenate([proj[..., :128], proj[..., 128:]], axis=2)
    p_mine[...] = proj.astype(BF)
    for copy in p_xc:
        copy.start()
    w_along_feat()
    total = p_mine[pl.ds(x * 4, 4)].astype(F32)
    for d in range(3):
        p_xc[d].wait_recv()
        total += p_x[d].astype(F32)
    p_xs[...] = total.astype(BF)
    for copy in p_yc:
        copy.start()
    w_last()
    total = p_xs[y].astype(F32)
    for d in range(3):
        p_yc[d].wait_recv()
        total += p_y[d].astype(F32)
    p_ys[...] = total.astype(BF)
    p_hc.start()

    for q in range(2):
        everything = [send(chip.at[q], land_b.at[q], ssem.at[q, k], rsem.at[q, 0, 0], buddy) for k in range(4)]
        everything[0].wait_send()
        everything[1].wait_send()
        everything[3].wait_send()

        @pl.when(hub)
        def _():
            everything[2].wait_send()
    for copy in [w_core, *w_xc, *w_yc, *p_xc, *p_yc]:
        copy.wait_send()

    @pl.when(c != hi)
    def _():
        w_hc.wait_send()

    @pl.when(c == hi)
    def _():
        for copy in w_zc:
            copy.wait_send()

    pltpu.make_async_copy(stage, eg_hbm, store_sem).wait()
    p_hc.wait_recv()
    total = p_ys[hi].astype(F32) + p_h[...].astype(F32)
    pg_ref[:, :128] = total[:8]
    pg_ref[:, 128:] = total[8:]
    p_hc.wait_send()


def local(embeds, proj_weight, hidden_weight, out_weight, cotangent):
    n, f, d = embeds.shape
    k = proj_weight.shape[1]
    h = hidden_weight.shape[1]
    dp_count = lax.axis_size("dp")
    mlp_scale = 4.0 / (n * dp_count)
    proj_scale = 1.0 / (n * dp_count * math.sqrt(d))
    vmem = pltpu.VMEM
    dma = pltpu.SemaphoreType.DMA
    anywhere = pl.BlockSpec(memory_space=pl.ANY)
    inside = pl.BlockSpec(memory_space=pltpu.VMEM)
    grad, proj, hid, out = pl.pallas_call(
        functools.partial(kernel, n),
        out_shape=(
            jax.ShapeDtypeStruct((n, f, d), BF),
            jax.ShapeDtypeStruct((8, f), F32),
            jax.ShapeDtypeStruct((8, h), F32),
            jax.ShapeDtypeStruct((16, d), F32),
        ),
        in_specs=[anywhere] * 5,
        out_specs=(anywhere, inside, inside, inside),
        scratch_shapes=[
            vmem((n, f, d), BF), vmem((f, k), BF), vmem((k, h), BF), vmem((h, d), BF), vmem((n, f, d), BF),
            vmem((k, f), BF), vmem((h, k), BF), vmem((h, d), BF),
            vmem((2, n, k, d), BF),
            vmem((2, n, k // 2, d), BF),
            vmem((2, n, k // 2, d), BF),
            vmem((2, n, k // 2, d), BF),
            vmem((2, n, k // 2, d), BF),
            vmem((2, n, k // 2, d), BF),
            vmem((2, n, k, d), BF),
            vmem((n, f, d), F32),
            vmem((n, f, d), BF),
            vmem((k, h), F32), vmem((h, d), F32), vmem((k, f), F32),
            vmem((16, 2, 16, 384), BF), vmem((16, 16, 384), BF), vmem((16, 16, 384), BF),
            vmem((3, 4, 16, 384), BF), vmem((4, 16, 384), BF),
            vmem((3, 16, 384), BF), vmem((16, 384), BF),
            vmem((16, 384), BF), vmem((16, 384), BF), vmem((4, 16, 384), BF),
            vmem((16, 2, 16, 128), BF), vmem((3, 4, 2, 16, 128), BF), vmem((4, 2, 16, 128), BF),
            vmem((3, 2, 16, 128), BF), vmem((2, 16, 128), BF), vmem((16, 128), BF),
            dma((5,)), dma, dma((2, 4)), dma((2, n, 4)),
            dma((15,)), dma((12,)), dma((7,)), dma((7,)),
        ],
        compiler_params=pltpu.CompilerParams(
            collective_id=0, has_side_effects=True, vmem_limit_bytes=40 * 1024 * 1024
        ),
    )(embeds, proj_weight, hidden_weight, out_weight, cotangent)
    return grad, proj.T * proj_scale, hid * mlp_scale, out * mlp_scale


def solution(mesh):
    placed = (P("dp", "feat", None), P("feat", None), P(), P(), P("dp", "feat", None))
    return jax.shard_map(
        local,
        mesh=mesh,
        in_specs=placed,
        out_specs=(P("dp", "feat", None), P("feat", "dp"), P("dp", None), P("dp", None)),
        check_vma=False,
    )
```

time: 864 us -> 73 us (0.08)
  the two profiles are of different devices: /device:TPU:32 before, /device:TPU:1 now
where the time goes in v1:
time: 73 us; the launch traced here: 72.8 us
  Pallas kernels  64.2 us (88%)
  local copies, waits for them, and re-layouts  6.17 us (8%)
  other arithmetic  1.81 us (2%)
    pallas_call x1, Pallas kernels, local(): pl.pallas_call(functools.partial(kernel, n), out_shape=(jax.ShapeDtypeStr...  64.2 us
    unnamed x11, local copies, waits for them, and re-layouts  6.17 us
    mul x3, other arithmetic, local(): return (grad, proj.T * proj_scale, hid * mlp_scale, out * mlp_scale)  1.81 us

profile of v1, /device:TPU:1, one launch (start us, length us, event | category | flops | bytes accessed | tf_op | source)
XLA Modules:
  0.0 72.8 jit_solution(5526295490180792692)
XLA Ops:
  0.6 0.0 copy-start
  0.6 1.2 %copy-done = bf16[16,256,128]{2,1,0:T(8,128)(2,1)S(1)} copy-done((bf16[16,256,128]{2,1,0:T(8,128)(2,1)S(1)}, bf16[16,256,128]{2,1,0:T(8,128)(2,1)}, u32[]{:S(2)}) %copy-start) | copy-done | bytes 1048600
  1.9 0.0 copy-start.1
  1.9 1.2 %copy-done.1 = bf16[16,256,128]{2,1,0:T(8,128)(2,1)S(1)} copy-done((bf16[16,256,128]{2,1,0:T(8,128)(2,1)S(1)}, bf16[16,256,128]{2,1,0:T(8,128)(2,1)}, u32[]{:S(2)}) %copy-start.1) | copy-done | bytes 1048600
  3.1 0.0 copy-start.2
  3.1 0.9 %copy-done.2 = bf16[256,512]{1,0:T(8,128)(2,1)S(1)} copy-done((bf16[256,512]{1,0:T(8,128)(2,1)S(1)}, bf16[256,512]{1,0:T(8,128)(2,1)}, u32[]{:S(2)}) %copy-start.2) | copy-done | bytes 262168
  4.0 0.0 copy-start.3
  4.0 0.9 %copy-done.3 = bf16[256,256]{1,0:T(8,128)(2,1)S(1)} copy-done((bf16[256,256]{1,0:T(8,128)(2,1)S(1)}, bf16[256,256]{1,0:T(8,128)(2,1)}, u32[]{:S(2)}) %copy-start.3) | copy-done | bytes 131096
  4.9 0.0 copy-start.4
  4.9 0.9 %copy-done.4 = bf16[512,128]{1,0:T(8,128)(2,1)S(1)} copy-done((bf16[512,128]{1,0:T(8,128)(2,1)S(1)}, bf16[512,128]{1,0:T(8,128)(2,1)}, u32[]{:S(2)}) %copy-start.4) | copy-done | bytes 131096
  5.8 64.2 %shard_map.84 = (bf16[16,256,128]{2,1,0:T(8,128)(2,1)S(1)}, f32[8,256]{1,0:T(8,128)S(1)}, f32[8,512]{1,0:T(8,128)S(1)}, f32[16,128]{1,0:T(8,128)S(1)}) custom-call(bf16[16,256,128]{2,1,0:T(8,128)(2,1)S(1)} %copy-done, bf16[256,256]{1,0:T(8,128)(2,1)S(1)} %copy-done.3, bf16[256,512]{1,0:T(8,128)(2,1)S(1)} %copy-done.2, bf16[512,128]{1,0:T(8,128)(2,1)S(1)} %copy-done.4, ...), custom_call_target="tpu_custom_call" | custom-call | tf_op jit(solution)/shard_map/pallas_call | solution.py:349
  70.0 0.6 multiply_bitcast_fusion
  70.6 0.6 broadcast_multiply_fusion.1
  71.2 0.6 broadcast_multiply_fusion
  71.8 1.0 %copy.10 = bf16[16,256,128]{2,1,0:T(8,128)(2,1)} copy(bf16[16,256,128]{2,1,0:T(8,128)(2,1)S(1)} %get-tuple-element.16) | data formatting | bytes 2097152
Async XLA Ops:
  0.6 1.2 %copy-start = (bf16[16,256,128]{2,1,0:T(8,128)(2,1)S(1)}, bf16[16,256,128]{2,1,0:T(8,128)(2,1)}, u32[]{:S(2)}) copy-start(bf16[16,256,128]{2,1,0:T(8,128)(2,1)} %e_hbm.1) | copy-start | bytes 3145732
  1.9 1.2 %copy-start.1 = (bf16[16,256,128]{2,1,0:T(8,128)(2,1)S(1)}, bf16[16,256,128]{2,1,0:T(8,128)(2,1)}, u32[]{:S(2)}) copy-start(bf16[16,256,128]{2,1,0:T(8,128)(2,1)} %c_hbm.1) | copy-start | bytes 3145732
  3.1 0.9 %copy-start.2 = (bf16[256,512]{1,0:T(8,128)(2,1)S(1)}, bf16[256,512]{1,0:T(8,128)(2,1)}, u32[]{:S(2)}) copy-start(bf16[256,512]{1,0:T(8,128)(2,1)} %w1_hbm.1) | copy-start | bytes 786436
  4.0 0.9 %copy-start.3 = (bf16[256,256]{1,0:T(8,128)(2,1)S(1)}, bf16[256,256]{1,0:T(8,128)(2,1)}, u32[]{:S(2)}) copy-start(bf16[256,256]{1,0:T(8,128)(2,1)} %p_hbm.1) | copy-start | bytes 393220
  4.9 0.9 %copy-start.4 = (bf16[512,128]{1,0:T(8,128)(2,1)S(1)}, bf16[512,128]{1,0:T(8,128)(2,1)}, u32[]{:S(2)}) copy-start(bf16[512,128]{1,0:T(8,128)(2,1)} %w2_hbm.1) | copy-start | bytes 393220

commit v2 on v1

v2 whole, which is shorter than its diff:
```python
import functools
import math

import jax
import jax.numpy as jnp
from jax import lax
from jax.experimental import pallas as pl
from jax.experimental.pallas import tpu as pltpu
from jax.sharding import PartitionSpec as P

MESH = pl.DeviceIdType.MESH
BF = jnp.bfloat16
F32 = jnp.float32

LAG_TOTAL = 2
LAG_SHARE = 4
LAG_MLP = 5
LAG2_FIRST = 6
LAG2_PAIR = 8
LAG2_TOTAL = 10
LAG2_SHARE = 12
LAG2_FINAL = 13


def nn(a, b):
    return lax.dot_general(a, b, (((1,), (0,)), ((), ())), preferred_element_type=F32)


def nt(a, b):
    return lax.dot_general(a, b, (((1,), (1,)), ((), ())), preferred_element_type=F32)


def tn(a, b):
    return lax.dot_general(a, b, (((0,), (0,)), ((), ())), preferred_element_type=F32)


def kernel(
    samples, e_hbm, p_hbm, w1_hbm, w2_hbm, c_hbm,
    eg_any, pg_ref, hg_ref, og_ref,
    e_ref, p_ref, w1_ref, w2_ref, c_ref, pt_ref, w1t_ref, w2h_ref,
    part, land_a, chip, land_b, pair, land_c, full,
    gacc, stage, hid_acc, out_acc, proj_acc,
    w_mine, w_buddy, w_chip, w_xy, w_plane, w_z, w_all,
    p_mine, p_land,
    load_sem, store_sem, ssem, rsem, wss, wrs, pss, prs, relay,
):
    pairs = samples // 2
    dp, ft = lax.axis_index("dp"), lax.axis_index("feat")
    x, y, hi = dp // 8, (dp // 2) % 4, dp % 2
    z, c = ft // 2, ft % 2
    hub = (z == 1) | (z == 2)
    outer = (z == 0) | (z == 3)
    half = (c + z) % 2
    mine = pl.ds(pl.multiple_of(half * 128, 128), 128)
    other = pl.ds(pl.multiple_of((1 - half) * 128, 128), 128)
    buddy = (dp, z * 2 + 1 - c)
    edge_z = jnp.where(z == 0, 1, jnp.where(z == 1, 0, jnp.where(z == 2, 3, 2)))
    edge = (dp, edge_z * 2 + 1 - c)
    across = (dp, (3 - z) * 2 + 1 - c)
    ring = (dp + 1 - 2 * hi, (3 - z) * 2 + c)
    third = (jnp.where(hub, dp, dp + 1 - 2 * hi), (3 - z) * 2 + jnp.where(hub, 1 - c, c))
    sides = [
        (((x + 1) % 4) * 8 + y * 2 + hi, ft),
        (((x + 3) % 4) * 8 + y * 2 + hi, ft),
        (x * 8 + ((y + 1) % 4) * 2 + hi, ft),
        (x * 8 + ((y + 3) % 4) * 2 + hi, ft),
    ]

    barrier = pltpu.get_barrier_semaphore()
    peers = [buddy, edge, third] + sides
    for peer in peers:
        pl.semaphore_signal(barrier, inc=1, device_id=peer, device_id_type=MESH)

    loads = [
        pltpu.make_async_copy(src, dst, load_sem.at[i])
        for i, (src, dst) in enumerate(
            ((p_hbm, p_ref), (e_hbm, e_ref), (w1_hbm, w1_ref), (w2_hbm, w2_ref), (c_hbm, c_ref))
        )
    ]
    for load in loads:
        load.start()

    def tell(r):
        for peer in sides:
            pl.semaphore_signal(relay.at[r], inc=1, device_id=peer, device_id_type=MESH)

    def hear(r):
        pl.semaphore_wait(relay.at[r], 4)

    def tell_ring(r):
        pl.semaphore_signal(relay.at[r], inc=1, device_id=ring, device_id_type=MESH)

    def hear_ring(r):
        pl.semaphore_wait(relay.at[r], 1)

    def send(src, dst, s_sem, r_sem, device):
        return pltpu.make_async_remote_copy(
            src_ref=src, dst_ref=dst, send_sem=s_sem, recv_sem=r_sem,
            device_id=device, device_id_type=MESH,
        )

    def to_buddy(q, s):
        return send(part.at[q, s, other], land_a.at[q, s], ssem.at[q, 0], rsem.at[q, s, 0], buddy)

    def to_hub(q, s):
        return send(chip.at[q, s], land_b.at[q, s], ssem.at[q, 1], rsem.at[q, s, 1], edge)

    def to_across(q, s):
        return send(pair.at[q, s], land_c.at[q, s], ssem.at[q, 1], rsem.at[q, s, 2], across)

    def to_outer(q, s):
        ref = full.at[q, s, mine]
        return send(ref, ref, ssem.at[q, 2], rsem.at[q, s, 1], edge)

    def share(q, s):
        ref = full.at[q, s, mine]
        return send(ref, ref, ssem.at[q, 3], rsem.at[q, s, 3], buddy)

    def first(q, s):
        to_buddy(q, s).wait_recv()
        chip[q, s] = (part[q, s, mine].astype(F32) + land_a[q, s].astype(F32)).astype(BF)
        to_hub(q, s).start()

    def paired(q, s):
        to_buddy(q, s).wait_recv()
        to_hub(q, s).wait_recv()
        total = part[q, s, mine].astype(F32) + land_a[q, s].astype(F32) + land_b[q, s].astype(F32)
        pair[q, s] = total.astype(BF)
        to_across(q, s).start()

    def totalled(q, s):
        to_across(q, s).wait_recv()
        full[q, s, mine] = (pair[q, s].astype(F32) + land_c[q, s].astype(F32)).astype(BF)
        to_outer(q, s).start()
        share(q, s).start()

    def shared(q, s):
        to_outer(q, s).wait_recv()
        share(q, s).start()

    loads[0].wait()
    pt_ref[...] = p_ref[...].T
    loads[1].wait()
    pl.semaphore_wait(barrier, len(peers))
    tell(0)

    def start_samples(i, carry):
        for s in [4 * i + j for j in range(4)]:
            part[0, s] = nn(pt_ref[...], e_ref[s]).astype(BF)
        for s in [4 * i + j for j in range(4)]:
            to_buddy(0, s).start()
        return carry

    lax.fori_loop(0, samples // 4, start_samples, 0)

    def first_samples(low, high):
        def body(s, carry):
            first(0, s)
            return carry

        lax.fori_loop(low, high, body, 0)

    @pl.when(outer)
    def _():
        for r in range(3):
            first_samples(4 * r, 4 * r + 4)
            hear(r)
            if r < 2:
                tell(r + 1)
        first_samples(12, samples)

    hid_acc[...] = jnp.zeros_like(hid_acc)
    out_acc[...] = jnp.zeros_like(out_acc)
    proj_acc[...] = jnp.zeros_like(proj_acc)
    for load in loads[2:]:
        load.wait()
    w1t_ref[...] = (w1_ref[...].T.astype(F32) * 0.5).astype(BF)
    w2h_ref[...] = (w2_ref[...].astype(F32) * 0.5).astype(BF)

    def mlp(both):
        for s in both:
            share(0, s).wait_recv()
        emb = [e_ref[s] for s in both]
        cot = [c_ref[s] for s in both]
        mix = [full[0, s] for s in both]
        inter = [nt(m, e).astype(BF) for m, e in zip(mix, emb)]
        u = [nn(w1t_ref[...], v) for v in inter]
        act_cot = [nt(w2h_ref[...], v) for v in cot]
        act, pre_cot = [], []
        for v, g in zip(u, act_cot):
            t = jnp.tanh(v)
            p = 1.0 + t
            a = v * p
            act.append(a.astype(BF))
            pre_cot.append((g * (p + a * (1.0 - t))).astype(BF))
        inter_cot = [nn(w1_ref[...], v).astype(BF) for v in pre_cot]
        for s, v, e in zip(both, inter_cot, emb):
            part[1, s] = nn(v, e).astype(BF)
        out_acc[...] += sum(nn(a, v) for a, v in zip(act, cot))
        hid_acc[...] += sum(nt(v, g) for v, g in zip(inter, pre_cot))
        for s, v, m, g in zip(both, inter_cot, mix, cot):
            gacc[s] = g.astype(F32) + tn(v, m)
        for s in both:
            to_buddy(1, s).start()

    def grad_of(both):
        for s in both:
            stage[s] = (gacc[s] + nn(p_ref[...], full[1, s])).astype(BF)
            pltpu.make_async_copy(stage.at[s], eg_any.at[s], store_sem).start()

    def proj_of(both):
        for s in both:
            share(1, s).wait_recv()
        return sum(nt(full[1, s], e_ref[s]) for s in both)

    def final(both):
        proj_acc[...] += proj_of(both)
        grad_of(both)

    w_core = send(w_mine.at[:, 1 - c], w_buddy, wss.at[0], wrs.at[0], buddy)
    place = x * 4 + y
    w_xyc = []
    for d in range(1, 16):
        there = (place + d) % 16
        w_xyc.append(send(w_chip.at[there], w_xy.at[d], wss.at[1], wrs.at[1], (there * 2 + hi, ft)))
    w_xy_all = send(w_chip.at[pl.ds(0, 15)], w_xy.at[pl.ds(1, 15)], wss.at[1], wrs.at[1], buddy)
    slot = hi * 4 + z
    w_zc = [
        send(w_plane, w_z.at[slot], wss.at[2], wrs.at[2], (place * 2 + c, ((z + d) % 4) * 2 + c))
        for d in range(4)
    ]

    def w_z_some(count):
        return send(w_z.at[pl.ds(0, count)], w_z.at[pl.ds(0, count)], wss.at[2], wrs.at[2], buddy)

    w_last = send(w_all, w_all, wss.at[3], wrs.at[3], buddy)

    def w_first():
        hid = hid_acc[...].reshape(16, 2, 8, 512)
        hid = jnp.concatenate([hid[..., :256], hid[..., 256:]], axis=2)
        w_mine[..., :256] = hid.astype(BF)
        w_mine[..., 256:] = out_acc[...].reshape(16, 2, 16, 128).astype(BF)
        w_core.start()

    def w_along_xy():
        w_core.wait_recv()
        w_chip[...] = (w_mine[:, c].astype(F32) + w_buddy[...].astype(F32)).astype(BF)
        for copy in w_xyc:
            copy.start()

    def w_along_z():
        w_xy_all.wait_recv()
        total = w_chip[place].astype(F32)
        for d in range(1, 16):
            total += w_xy[d].astype(F32)
        w_plane[...] = total.astype(BF)
        for copy in w_zc[1:]:
            copy.start()

        @pl.when(c != hi)
        def _():
            w_zc[0].start()

        @pl.when(c == hi)
        def _():
            w_z[slot] = total.astype(BF)

    def w_share():
        @pl.when(c == hi)
        def _():
            w_z_some(7).wait_recv()
            total = w_z[0].astype(F32)
            for d in range(1, 8):
                total += w_z[d].astype(F32)
            w_all[...] = total
            w_last.start()

    def step(t, carry):
        def on(lag, who, act, count=pairs):
            @pl.when((t >= lag) & (t < lag + count) & who)
            def _():
                s = (t - lag) * 2
                act([s, s + 1])

        def each(act):
            def run(both):
                for s in both:
                    act(s)

            return run

        def once(at, who, act):
            @pl.when((t == at) & who)
            def _():
                act()

        def pass_on(r):
            hear(r)
            if r < 2:
                tell(r + 1)

        everyone = t >= 0
        for r in range(3):
            once(2 * r, hub, functools.partial(pass_on, r))
        on(0, hub, each(functools.partial(paired, 0)))
        on(LAG_TOTAL, hub, each(functools.partial(totalled, 0)))
        on(LAG_SHARE, outer, each(functools.partial(shared, 0)))
        on(LAG_MLP, everyone, mlp)
        once(LAG_MLP + pairs, everyone, w_first)
        once(LAG_MLP, outer, lambda: tell_ring(3))
        once(LAG_MLP + pairs - 2, outer, lambda: tell_ring(4))
        once(LAG2_FIRST, outer, lambda: hear_ring(3))
        once(LAG2_FIRST + pairs - 2, outer, lambda: hear_ring(4))
        on(LAG2_FIRST, outer, each(functools.partial(first, 1)))
        on(LAG2_PAIR, hub, each(functools.partial(paired, 1)))
        on(LAG2_TOTAL, hub, each(functools.partial(totalled, 1)))
        on(LAG2_SHARE, outer, each(functools.partial(shared, 1)))
        once(LAG_MLP + pairs + 1, everyone, w_along_xy)
        once(LAG_MLP + pairs + 6, everyone, w_along_z)
        on(LAG2_FINAL, everyone, final, pairs - 1)
        return carry

    lax.fori_loop(0, pairs - 1 + LAG2_FINAL, step, 0)

    last = [samples - 2, samples - 1]
    proj = (proj_acc[...] + proj_of(last)).reshape(32, 8, 256)
    proj = jnp.concatenate([proj[..., :128], proj[..., 128:]], axis=1)
    p_mine[...] = proj.astype(BF)
    p_copies = []
    for d in range(1, 32):
        there = (dp + d) % 32
        p_copies.append(send(p_mine.at[there], p_land.at[d], pss, prs, (there, ft)))
    for copy in p_copies:
        copy.start()
    p_all = send(p_mine.at[pl.ds(0, 31)], p_land.at[pl.ds(1, 31)], pss, prs, buddy)
    grad_of(last)
    w_share()

    for q in range(2):
        sent = [send(chip.at[q], land_b.at[q], ssem.at[q, k], rsem.at[q, 0, 0], buddy) for k in range(4)]
        for k in (0, 1, 3):
            sent[k].wait_send()

        @pl.when(hub)
        def _():
            sent[2].wait_send()
    w_core.wait_send()
    w_xy_all.wait_send()

    @pl.when(c != hi)
    def _():
        w_z_some(4).wait_send()
        w_last.wait_recv()

    @pl.when(c == hi)
    def _():
        w_z_some(3).wait_send()
        w_last.wait_send()

    hg_ref[:, :256] = w_all[:8, :256]
    hg_ref[:, 256:] = w_all[8:, :256]
    og_ref[...] = w_all[:, 256:]
    pltpu.make_async_copy(stage, eg_any, store_sem).wait()
    p_all.wait_recv()
    total = p_mine[dp].astype(F32)
    for d in range(1, 32):
        total += p_land[d].astype(F32)
    pg_ref[:, :128] = total[:8]
    pg_ref[:, 128:] = total[8:]
    p_all.wait_send()


def finish(scales, eg_in, pg_in, hg_in, og_in, eg_out, pg_out, hg_out, og_out, sem):
    rows = eg_in.shape[0] // 4
    copies = [
        pltpu.make_async_copy(eg_in.at[pl.ds(i * rows, rows)], eg_out.at[pl.ds(i * rows, rows)], sem.at[i])
        for i in range(4)
    ]
    for copy in copies:
        copy.start()
    pg_out[...] = pg_in[...] * scales[0]
    hg_out[...] = hg_in[...] * scales[1]
    og_out[...] = og_in[...] * scales[1]
    for copy in copies:
        copy.wait()


def local(embeds, proj_weight, hidden_weight, out_weight, cotangent):
    n, f, d = embeds.shape
    k = proj_weight.shape[1]
    h = hidden_weight.shape[1]
    dp_count = lax.axis_size("dp")
    mlp_scale = 4.0 / (n * dp_count)
    proj_scale = 1.0 / (n * dp_count * math.sqrt(d))
    vmem = pltpu.VMEM
    dma = pltpu.SemaphoreType.DMA
    hbm = pl.BlockSpec(memory_space=pltpu.HBM)
    anywhere = pl.BlockSpec(memory_space=pl.ANY)
    inside = pl.BlockSpec(memory_space=pltpu.VMEM)
    shapes = (
        jax.ShapeDtypeStruct((n, f, d), BF),
        jax.ShapeDtypeStruct((8, f), F32),
        jax.ShapeDtypeStruct((8, h), F32),
        jax.ShapeDtypeStruct((16, d), F32),
    )
    results = pl.pallas_call(
        functools.partial(kernel, n),
        out_shape=shapes,
        in_specs=[hbm] * 5,
        out_specs=(anywhere, inside, inside, inside),
        scratch_shapes=[
            vmem((n, f, d), BF), vmem((f, k), BF), vmem((k, h), BF), vmem((h, d), BF), vmem((n, f, d), BF),
            vmem((k, f), BF), vmem((h, k), BF), vmem((h, d), BF),
            vmem((2, n, k, d), BF),
            vmem((2, n, k // 2, d), BF),
            vmem((2, n, k // 2, d), BF),
            vmem((2, n, k // 2, d), BF),
            vmem((2, n, k // 2, d), BF),
            vmem((2, n, k // 2, d), BF),
            vmem((2, n, k, d), BF),
            vmem((n, f, d), F32),
            vmem((n, f, d), BF),
            vmem((k, h), F32), vmem((h, d), F32), vmem((k, f), F32),
            vmem((16, 2, 16, 384), BF), vmem((16, 16, 384), BF), vmem((16, 16, 384), BF),
            vmem((16, 16, 384), BF), vmem((16, 384), BF), vmem((8, 16, 384), BF), vmem((16, 384), F32),
            vmem((32, 16, 128), BF), vmem((32, 16, 128), BF),
            dma((5,)), dma, dma((2, 4)), dma((2, n, 4)),
            dma((4,)), dma((4,)), dma, dma, pltpu.SemaphoreType.REGULAR((5,)),
        ],
        compiler_params=pltpu.CompilerParams(
            collective_id=0, has_side_effects=True, vmem_limit_bytes=40 * 1024 * 1024
        ),
    )(embeds, proj_weight, hidden_weight, out_weight, cotangent)
    grad, proj, hid, out = pl.pallas_call(
        functools.partial(finish, (proj_scale, mlp_scale)),
        out_shape=shapes,
        in_specs=[anywhere, inside, inside, inside],
        out_specs=(hbm, inside, inside, inside),
        scratch_shapes=[dma((4,))],
    )(*results)
    return grad, proj.T, hid, out


def solution(mesh):
    placed = (P("dp", "feat", None), P("feat", None), P(), P(), P("dp", "feat", None))
    return jax.shard_map(
        local,
        mesh=mesh,
        in_specs=placed,
        out_specs=(P("dp", "feat", None), P("feat", "dp"), P("dp", None), P("dp", None)),
        check_vma=False,
    )
```

time: 73 us -> 99.4 us (1.36)
  Pallas kernels: 64.2 us -> 90.5 us
  other arithmetic: 1.81 us -> 0 us
  local copies, waits for them, and re-layouts: 6.17 us -> 7.96 us
    pallas_call x1 -> x2, Pallas kernels: 64.2 us -> 90.5 us  [the longest x1 56.2 us: local(): pl.pallas_call(functools.partial(kernel, n), out_shape=shapes, in_specs=[...]
    mul x3 -> x0, other arithmetic: 1.81 us -> none  [local(): return (grad, proj.T * proj_scale, hid * mlp_scale, out * mlp_scale)]
    unnamed x11 -> x18, local copies, waits for them, and re-layouts: 6.17 us -> 7.96 us
where the time goes in v2:
time: 99.4 us; the launch traced here: 99.1 us
  Pallas kernels  90.5 us (91%)
  local copies, waits for them, and re-layouts  7.96 us (8%)
    pallas_call x1, Pallas kernels, local(): pl.pallas_call(functools.partial(kernel, n), out_shape=shapes, in_specs=[...  56.2 us
    pallas_call x1, Pallas kernels, local(): pl.pallas_call(functools.partial(finish, (proj_scale, mlp_scale)), out_sh...  34.2 us
    unnamed x18, local copies, waits for them, and re-layouts  7.96 us

profile of v2, /device:TPU:1, one launch (start us, length us, event | category | flops | bytes accessed | tf_op | source)
XLA Modules:
  0.0 99.1 jit_solution(10654814446530057860)
XLA Ops:
  0.6 0.0 copy-start
  0.6 1.2 %copy-done = bf16[16,256,128]{2,1,0:T(8,128)(2,1)S(1)} copy-done((bf16[16,256,128]{2,1,0:T(8,128)(2,1)S(1)}, bf16[16,256,128]{2,1,0:T(8,128)(2,1)}, u32[]{:S(2)}) %copy-start) | copy-done | bytes 1048600
  1.9 0.0 copy-start.1
  1.9 1.2 %copy-done.1 = bf16[16,256,128]{2,1,0:T(8,128)(2,1)S(1)} copy-done((bf16[16,256,128]{2,1,0:T(8,128)(2,1)S(1)}, bf16[16,256,128]{2,1,0:T(8,128)(2,1)}, u32[]{:S(2)}) %copy-start.1) | copy-done | bytes 1048600
  3.1 0.0 copy-start.3
  3.1 0.9 copy-done.3
  4.0 0.0 copy-start.4
  4.0 0.9 copy-done.4
  4.9 0.0 copy-start.5
  4.9 0.9 copy-done.5
  5.8 56.2 %shard_map.84 = (bf16[16,256,128]{2,1,0:T(8,128)(2,1)S(1)}, f32[8,256]{1,0:T(8,128)S(1)}, f32[8,512]{1,0:T(8,128)S(1)}, f32[16,128]{1,0:T(8,128)S(1)}) custom-call(bf16[16,256,128]{2,1,0:T(8,128)(2,1)S(1)} %copy-done, bf16[256,256]{1,0:T(8,128)(2,1)S(1)} %copy-done.4, bf16[256,512]{1,0:T(8,128)(2,1)S(1)} %copy-done.3, bf16[512,128]{1,0:T(8,128)(2,1)S(1)} %copy-done.5, ...), custom_call_target="tpu_custom_call" | custom-call | tf_op jit(solution)/shard_map/pallas_call | solution.py:406
  62.1 0.0 copy-start.2
  62.1 1.0 copy-done.2
  63.1 0.0 copy-start.6
  63.1 0.6 copy-done.6
  63.7 0.0 copy-start.7
  63.7 0.6 copy-done.7
  64.3 0.0 copy-start.8
  64.3 0.6 copy-done.8
  64.9 34.2 %shard_map.85 = (bf16[16,256,128]{2,1,0:T(8,128)(2,1)}, f32[8,256]{1,0:T(8,128)}, f32[8,512]{1,0:T(8,128)}, f32[16,128]{1,0:T(8,128)}) custom-call(bf16[16,256,128]{2,1,0:T(8,128)(2,1)} %copy-done.2, f32[8,256]{1,0:T(8,128)} %copy-done.7, f32[8,512]{1,0:T(8,128)} %copy-done.6, f32[16,128]{1,0:T(8,128)} %copy-done.8), custom_call_target="tpu_custom_call" | custom-call | tf_op jit(solution)/shard_map/pallas_call | solution.py:434
Async XLA Ops:
  0.6 1.2 %copy-start = (bf16[16,256,128]{2,1,0:T(8,128)(2,1)S(1)}, bf16[16,256,128]{2,1,0:T(8,128)(2,1)}, u32[]{:S(2)}) copy-start(bf16[16,256,128]{2,1,0:T(8,128)(2,1)} %e_hbm.1) | copy-start | bytes 3145732
  1.9 1.2 %copy-start.1 = (bf16[16,256,128]{2,1,0:T(8,128)(2,1)S(1)}, bf16[16,256,128]{2,1,0:T(8,128)(2,1)}, u32[]{:S(2)}) copy-start(bf16[16,256,128]{2,1,0:T(8,128)(2,1)} %c_hbm.1) | copy-start | bytes 3145732
  3.1 0.9 copy-start.3
  4.0 0.9 copy-start.4
  4.9 0.9 copy-start.5
  62.1 1.0 copy-start.2
  63.1 0.6 copy-start.6
  63.7 0.6 copy-start.7
  64.3 0.6 copy-start.8

commit v3 on v2

--- a/solution.py
+++ b/solution.py
@@ -35,7 +35,7 @@
 
 
 def kernel(
-    samples, e_hbm, p_hbm, w1_hbm, w2_hbm, c_hbm,
+    samples, proj_scale, mlp_scale, e_hbm, p_hbm, w1_hbm, w2_hbm, c_hbm,
     eg_any, pg_ref, hg_ref, og_ref,
     e_ref, p_ref, w1_ref, w2_ref, c_ref, pt_ref, w1t_ref, w2h_ref,
     part, land_a, chip, land_b, pair, land_c, full,
@@ -357,32 +357,35 @@
         w_z_some(3).wait_send()
         w_last.wait_send()
 
-    hg_ref[:, :256] = w_all[:8, :256]
-    hg_ref[:, 256:] = w_all[8:, :256]
-    og_ref[...] = w_all[:, 256:]
+    hg_ref[:, :256] = w_all[:8, :256] * mlp_scale
+    hg_ref[:, 256:] = w_all[8:, :256] * mlp_scale
+    og_ref[...] = w_all[:, 256:] * mlp_scale
     pltpu.make_async_copy(stage, eg_any, store_sem).wait()
     p_all.wait_recv()
     total = p_mine[dp].astype(F32)
     for d in range(1, 32):
         total += p_land[d].astype(F32)
-    pg_ref[:, :128] = total[:8]
-    pg_ref[:, 128:] = total[8:]
+    pg_ref[:, :128] = total[:8] * proj_scale
+    pg_ref[:, 128:] = total[8:] * proj_scale
     p_all.wait_send()
 
 
-def finish(scales, eg_in, pg_in, hg_in, og_in, eg_out, pg_out, hg_out, og_out, sem):
-    rows = eg_in.shape[0] // 4
-    copies = [
-        pltpu.make_async_copy(eg_in.at[pl.ds(i * rows, rows)], eg_out.at[pl.ds(i * rows, rows)], sem.at[i])
-        for i in range(4)
-    ]
-    for copy in copies:
-        copy.start()
-    pg_out[...] = pg_in[...] * scales[0]
-    hg_out[...] = hg_in[...] * scales[1]
-    og_out[...] = og_in[...] * scales[1]
-    for copy in copies:
-        copy.wait()
+def finish(eg_in, pg_in, hg_in, og_in, eg_out, pg_out, hg_out, og_out, eg, pg, hg, og, in_sem, out_sem):
+    parts = in_sem.shape[0] - 3
+    rows = eg.shape[0] // parts
+    moves = [(pg_in, pg, pg_out), (hg_in, hg, hg_out), (og_in, og, og_out)]
+    for i in range(parts):
+        some = pl.ds(i * rows, rows)
+        moves.append((eg_in.at[some], eg.at[some], eg_out.at[some]))
+    loads = [pltpu.make_async_copy(m[0], m[1], in_sem.at[i]) for i, m in enumerate(moves)]
+    stores = [pltpu.make_async_copy(m[1], m[2], out_sem.at[i]) for i, m in enumerate(moves)]
+    for load in loads:
+        load.start()
+    for load, store in zip(loads, stores):
+        load.wait()
+        store.start()
+    for store in stores:
+        store.wait()
 
 
 def local(embeds, proj_weight, hidden_weight, out_weight, cotangent):
@@ -404,7 +407,7 @@
         jax.ShapeDtypeStruct((16, d), F32),
     )
     results = pl.pallas_call(
-        functools.partial(kernel, n),
+        functools.partial(kernel, n, proj_scale, mlp_scale),
         out_shape=shapes,
         in_specs=[hbm] * 5,
         out_specs=(anywhere, inside, inside, inside),
@@ -428,15 +431,16 @@
             dma((4,)), dma((4,)), dma, dma, pltpu.SemaphoreType.REGULAR((5,)),
         ],
         compiler_params=pltpu.CompilerParams(
-            collective_id=0, has_side_effects=True, vmem_limit_bytes=40 * 1024 * 1024
+            collective_id=0, has_side_effects=True, vmem_limit_bytes=60 * 1024 * 1024
         ),
     )(embeds, proj_weight, hidden_weight, out_weight, cotangent)
     grad, proj, hid, out = pl.pallas_call(
-        functools.partial(finish, (proj_scale, mlp_scale)),
+        finish,
         out_shape=shapes,
-        in_specs=[anywhere, inside, inside, inside],
-        out_specs=(hbm, inside, inside, inside),
-        scratch_shapes=[dma((4,))],
+        in_specs=[hbm] * 4,
+        out_specs=(hbm,) * 4,
+        scratch_shapes=[vmem(v.shape, v.dtype) for v in shapes] + [dma((7,)), dma((7,))],
+        compiler_params=pltpu.CompilerParams(vmem_limit_bytes=60 * 1024 * 1024),
     )(*results)
     return grad, proj.T, hid, out
 

time: 99.4 us -> 59.6 us (0.60)
  Pallas kernels: 90.5 us -> 58.8 us
  local copies, waits for them, and re-layouts: 7.96 us -> 0 us
    pallas_call x2, Pallas kernels: 90.5 us -> 58.8 us  [the longest x1 56.8 us: local(): pl.pallas_call(functools.partial(kernel, n, proj_scale, mlp_scale), out_s...]
    unnamed x18 -> x0, local copies, waits for them, and re-layouts: 7.96 us -> none
where the time goes in v3:
time: 59.6 us; the launch traced here: 59.5 us
  Pallas kernels  58.8 us (99%)
  between operations  0.64 us (1%)
    pallas_call x1, Pallas kernels, local(): pl.pallas_call(functools.partial(kernel, n, proj_scale, mlp_scale), out_s...  56.8 us
    pallas_call x1, Pallas kernels, local(): pl.pallas_call(finish, out_shape=shapes, in_specs=[hbm] * 4, out_specs=(h...  2.08 us

profile of v3, /device:TPU:1, one launch (start us, length us, event | category | flops | bytes accessed | tf_op | source)
XLA Modules:
  0.0 59.5 jit_solution(2853176675484596162)
XLA Ops:
  0.6 56.8 %shard_map.84 = (bf16[16,256,128]{2,1,0:T(8,128)(2,1)}, f32[8,256]{1,0:T(8,128)}, f32[8,512]{1,0:T(8,128)}, f32[16,128]{1,0:T(8,128)}) custom-call(bf16[16,256,128]{2,1,0:T(8,128)(2,1)} %e_hbm.1, bf16[256,256]{1,0:T(8,128)(2,1)} %p_hbm.1, bf16[256,512]{1,0:T(8,128)(2,1)} %w1_hbm.1, bf16[512,128]{1,0:T(8,128)(2,1)} %w2_hbm.1, bf16[16,256,128]{2,1,0:T(8,128)(2,1)} %c_hbm.1), custom_call_target="tpu_custom_call" | custom-call | tf_op jit(solution)/shard_map/pallas_call | solution.py:409
  57.4 2.1 %shard_map.85 = (bf16[16,256,128]{2,1,0:T(8,128)(2,1)}, f32[8,256]{1,0:T(8,128)}, f32[8,512]{1,0:T(8,128)}, f32[16,128]{1,0:T(8,128)}) custom-call(bf16[16,256,128]{2,1,0:T(8,128)(2,1)} %get-tuple-element.12.eg_in, f32[8,256]{1,0:T(8,128)} %get-tuple-element.13.pg_in, f32[8,512]{1,0:T(8,128)} %get-tuple-element.14.hg_in, f32[16,128]{1,0:T(8,128)} %get-tuple-element.15.og_in), custom_call_target="tpu_custom_call" | custom-call | tf_op jit(solution)/shard_map/pallas_call | solution.py:437

commit v4 on v3

--- a/solution.py
+++ b/solution.py
@@ -1,4 +1,5 @@
 import functools
+import itertools
 import math
 
 import jax
@@ -12,14 +13,13 @@
 BF = jnp.bfloat16
 F32 = jnp.float32
 
-LAG_TOTAL = 2
-LAG_SHARE = 4
-LAG_MLP = 5
-LAG2_FIRST = 6
-LAG2_PAIR = 8
-LAG2_TOTAL = 10
-LAG2_SHARE = 12
-LAG2_FINAL = 13
+LAG_TOTAL = 5
+LAG_SHARE = 10
+LAG_MLP = 12
+LAG2_FIRST = 15
+LAG2_PAIR = 20
+LAG2_TOTAL = 25
+LAG2_SHARE = 30
 
 
 def nn(a, b):
@@ -39,10 +39,10 @@
     eg_any, pg_ref, hg_ref, og_ref,
     e_ref, p_ref, w1_ref, w2_ref, c_ref, pt_ref, w1t_ref, w2h_ref,
     part, land_a, chip, land_b, pair, land_c, full,
-    gacc, stage, hid_acc, out_acc, proj_acc,
+    act_cot, icot, inters, acts, pre_cots, stage, hid_acc, out_acc, proj_acc,
     w_mine, w_buddy, w_chip, w_xy, w_plane, w_z, w_all,
     p_mine, p_land,
-    load_sem, store_sem, ssem, rsem, wss, wrs, pss, prs, relay,
+    e2_ref, load_sem, store_sem, ssem, rsem, wss, wrs, pss, prs, relay,
 ):
     pairs = samples // 2
     dp, ft = lax.axis_index("dp"), lax.axis_index("feat")
@@ -51,8 +51,9 @@
     hub = (z == 1) | (z == 2)
     outer = (z == 0) | (z == 3)
     half = (c + z) % 2
+    hi_half = dp // 16
+    other = pl.ds(pl.multiple_of((1 - half) * 128, 128), 128)
     mine = pl.ds(pl.multiple_of(half * 128, 128), 128)
-    other = pl.ds(pl.multiple_of((1 - half) * 128, 128), 128)
     buddy = (dp, z * 2 + 1 - c)
     edge_z = jnp.where(z == 0, 1, jnp.where(z == 1, 0, jnp.where(z == 2, 3, 2)))
     edge = (dp, edge_z * 2 + 1 - c)
@@ -66,6 +67,8 @@
         (x * 8 + ((y + 3) % 4) * 2 + hi, ft),
     ]
 
+    opposite = [(((x + 2) % 4) * 8 + y * 2 + hi, ft), (x * 8 + ((y + 2) % 4) * 2 + hi, ft)]
+
     barrier = pltpu.get_barrier_semaphore()
     peers = [buddy, edge, third] + sides
     for peer in peers:
@@ -77,15 +80,15 @@
             ((p_hbm, p_ref), (e_hbm, e_ref), (w1_hbm, w1_ref), (w2_hbm, w2_ref), (c_hbm, c_ref))
         )
     ]
-    for load in loads:
+    for load in loads[:2]:
         load.start()
 
     def tell(r):
-        for peer in sides:
+        for peer in (sides, opposite)[r]:
             pl.semaphore_signal(relay.at[r], inc=1, device_id=peer, device_id_type=MESH)
 
     def hear(r):
-        pl.semaphore_wait(relay.at[r], 4)
+        pl.semaphore_wait(relay.at[r], (4, 2)[r])
 
     def tell_ring(r):
         pl.semaphore_signal(relay.at[r], inc=1, device_id=ring, device_id_type=MESH)
@@ -98,6 +101,8 @@
             src_ref=src, dst_ref=dst, send_sem=s_sem, recv_sem=r_sem,
             device_id=device, device_id_type=MESH,
         )
+
+    swap = send(e_ref, e2_ref, ssem.at[0, 4], rsem.at[0, 0, 4], buddy)
 
     def to_buddy(q, s):
         return send(part.at[q, s, other], land_a.at[q, s], ssem.at[q, 0], rsem.at[q, s, 0], buddy)
@@ -141,17 +146,23 @@
     loads[0].wait()
     pt_ref[...] = p_ref[...].T
     loads[1].wait()
-    pl.semaphore_wait(barrier, len(peers))
-    tell(0)
+    for load in loads[2:]:
+        load.start()
 
     def start_samples(i, carry):
         for s in [4 * i + j for j in range(4)]:
             part[0, s] = nn(pt_ref[...], e_ref[s]).astype(BF)
-        for s in [4 * i + j for j in range(4)]:
-            to_buddy(0, s).start()
         return carry
 
+    def send_samples(s, carry):
+        to_buddy(0, s).start()
+        return carry
+
     lax.fori_loop(0, samples // 4, start_samples, 0)
+    pl.semaphore_wait(barrier, len(peers))
+    lax.fori_loop(0, samples, send_samples, 0)
+    tell(0)
+    swap.start()
 
     def first_samples(low, high):
         def body(s, carry):
@@ -162,59 +173,67 @@
 
     @pl.when(outer)
     def _():
-        for r in range(3):
-            first_samples(4 * r, 4 * r + 4)
-            hear(r)
-            if r < 2:
-                tell(r + 1)
-        first_samples(12, samples)
+        first_samples(0, 6)
 
     hid_acc[...] = jnp.zeros_like(hid_acc)
     out_acc[...] = jnp.zeros_like(out_acc)
     proj_acc[...] = jnp.zeros_like(proj_acc)
+    for ref in (*inters, *acts, *pre_cots):
+        ref[...] = jnp.zeros_like(ref)
     for load in loads[2:]:
         load.wait()
     w1t_ref[...] = (w1_ref[...].T.astype(F32) * 0.5).astype(BF)
     w2h_ref[...] = (w2_ref[...].astype(F32) * 0.5).astype(BF)
 
-    def mlp(both):
-        for s in both:
-            share(0, s).wait_recv()
-        emb = [e_ref[s] for s in both]
-        cot = [c_ref[s] for s in both]
-        mix = [full[0, s] for s in both]
-        inter = [nt(m, e).astype(BF) for m, e in zip(mix, emb)]
-        u = [nn(w1t_ref[...], v) for v in inter]
-        act_cot = [nt(w2h_ref[...], v) for v in cot]
-        act, pre_cot = [], []
-        for v, g in zip(u, act_cot):
-            t = jnp.tanh(v)
-            p = 1.0 + t
-            a = v * p
-            act.append(a.astype(BF))
-            pre_cot.append((g * (p + a * (1.0 - t))).astype(BF))
-        inter_cot = [nn(w1_ref[...], v).astype(BF) for v in pre_cot]
-        for s, v, e in zip(both, inter_cot, emb):
-            part[1, s] = nn(v, e).astype(BF)
-        out_acc[...] += sum(nn(a, v) for a, v in zip(act, cot))
-        hid_acc[...] += sum(nt(v, g) for v, g in zip(inter, pre_cot))
-        for s, v, m, g in zip(both, inter_cot, mix, cot):
-            gacc[s] = g.astype(F32) + tn(v, m)
-        for s in both:
-            to_buddy(1, s).start()
+    def act_cots(i, carry):
+        for s in (2 * i, 2 * i + 1):
+            act_cot[s] = nt(w2h_ref[...], c_ref[s])
+        return carry
+
+    lax.fori_loop(0, pairs, act_cots, 0)
+
+    @pl.when(outer)
+    def _():
+        hear(0)
+        tell(1)
+        first_samples(6, 12)
+        hear(1)
+        first_samples(12, samples)
+
+    def mlp(s, now, before):
+        r = jnp.maximum(s - 1, 0)
+        s = jnp.minimum(s, samples - 1)
+        inter_cot = nn(w1_ref[...], pre_cots[before][...]).astype(BF)
+        icot[r] = inter_cot
+        inter = nt(full[0, s], e_ref[s]).astype(BF)
+        hid_acc[...] += nt(inters[before][...], pre_cots[before][...])
+        u = nn(w1t_ref[...], inter)
+        out_acc[...] += nn(acts[before][...], c_ref[r])
+        t = jnp.tanh(u)
+        p = 1.0 + t
+        a = u * p
+        inters[now][...] = inter
+        acts[now][...] = a.astype(BF)
+        pre_cots[now][...] = (act_cot[s] * (p + a * (1.0 - t))).astype(BF)
+        part[1, r] = nn(inter_cot, e_ref[r]).astype(BF)
 
     def grad_of(both):
         for s in both:
-            stage[s] = (gacc[s] + nn(p_ref[...], full[1, s])).astype(BF)
+            total = tn(icot[s], full[0, s]) + nn(p_ref[...], full[1, s])
+            stage[s] = (c_ref[s].astype(F32) + total).astype(BF)
             pltpu.make_async_copy(stage.at[s], eg_any.at[s], store_sem).start()
 
-    def proj_of(both):
+    def proj_of(own, both):
+        emb = e_ref if own else e2_ref
+        return sum(nt(full[1, s, mine], emb[s]) for s in both)
+
+    def proj_some(both):
+        for i in range(2):
+            proj_acc[i] += proj_of(i == 0, both)
+
+    def final(both):
         for s in both:
             share(1, s).wait_recv()
-        return sum(nt(full[1, s], e_ref[s]) for s in both)
-
-    def final(both):
-        proj_acc[...] += proj_of(both)
         grad_of(both)
 
     w_core = send(w_mine.at[:, 1 - c], w_buddy, wss.at[0], wrs.at[0], buddy)
@@ -275,64 +294,117 @@
             w_all[...] = total
             w_last.start()
 
-    def step(t, carry):
-        def on(lag, who, act, count=pairs):
-            @pl.when((t >= lag) & (t < lag + count) & who)
-            def _():
-                s = (t - lag) * 2
-                act([s, s + 1])
-
-        def each(act):
-            def run(both):
-                for s in both:
-                    act(s)
-
-            return run
-
-        def once(at, who, act):
-            @pl.when((t == at) & who)
-            def _():
-                act()
-
-        def pass_on(r):
-            hear(r)
-            if r < 2:
-                tell(r + 1)
-
-        everyone = t >= 0
-        for r in range(3):
-            once(2 * r, hub, functools.partial(pass_on, r))
-        on(0, hub, each(functools.partial(paired, 0)))
-        on(LAG_TOTAL, hub, each(functools.partial(totalled, 0)))
-        on(LAG_SHARE, outer, each(functools.partial(shared, 0)))
-        on(LAG_MLP, everyone, mlp)
-        once(LAG_MLP + pairs, everyone, w_first)
-        once(LAG_MLP, outer, lambda: tell_ring(3))
-        once(LAG_MLP + pairs - 2, outer, lambda: tell_ring(4))
-        once(LAG2_FIRST, outer, lambda: hear_ring(3))
-        once(LAG2_FIRST + pairs - 2, outer, lambda: hear_ring(4))
-        on(LAG2_FIRST, outer, each(functools.partial(first, 1)))
-        on(LAG2_PAIR, hub, each(functools.partial(paired, 1)))
-        on(LAG2_TOTAL, hub, each(functools.partial(totalled, 1)))
-        on(LAG2_SHARE, outer, each(functools.partial(shared, 1)))
-        once(LAG_MLP + pairs + 1, everyone, w_along_xy)
-        once(LAG_MLP + pairs + 6, everyone, w_along_z)
-        on(LAG2_FINAL, everyone, final, pairs - 1)
+    def when(condition, act, *args):
+        pl.when(condition)(lambda: act(*args))
+
+    def within(u, lag, act, *args):
+        when((u >= lag) & (u < lag + samples), act, *args, u - lag)
+
+    def fill(u, carry):
+        @pl.when(hub)
+        def _():
+            when(u == 0, hear, 0)
+            when(u == 0, tell, 1)
+            when(u == 8, hear, 1)
+            paired(0, u)
+            when(u >= LAG_TOTAL, totalled, 0, u - LAG_TOTAL)
+
+        when(outer & (u >= LAG_SHARE), shared, 0, u - LAG_SHARE)
         return carry
 
-    lax.fori_loop(0, pairs - 1 + LAG2_FINAL, step, 0)
-
+    def middle(s, now):
+        u = s + LAG_MLP
+
+        @pl.when(hub)
+        def _():
+            within(u, 0, paired, 0)
+            within(u, LAG_TOTAL, totalled, 0)
+
+        @pl.when(outer)
+        def _():
+            within(u, LAG_SHARE, shared, 0)
+
+        when(s < samples, lambda: share(0, s).wait_recv())
+        mlp(s, now, 1 - now)
+        when(s > 0, lambda: to_buddy(1, s - 1).start())
+
+        @pl.when(outer)
+        def _():
+            when(s == 0, tell_ring, 2)
+            when(s == 8, hear_ring, 2)
+            when(s == 13, tell_ring, 3)
+            within(u, LAG2_FIRST, first, 1)
+
+        @pl.when(hub)
+        def _():
+            within(u, LAG2_PAIR, paired, 1)
+            within(u, LAG2_TOTAL, totalled, 1)
+
+    def middle_two(i, carry):
+        middle(2 * i, 0)
+        when(i < pairs, middle, 2 * i + 1, 1)
+        return carry
+
+    def drain(u, carry):
+        done = samples + LAG_MLP + 1
+        when(u == done, w_first)
+        when(u == done, swap.wait_recv)
+        when(u == done + 2, w_along_xy)
+
+        @pl.when(outer)
+        def _():
+            when(u == LAG2_FIRST + samples - 1, hear_ring, 3)
+            within(u, LAG2_FIRST, first, 1)
+            when(u >= LAG2_SHARE, shared, 1, u - LAG2_SHARE)
+
+        @pl.when(hub)
+        def _():
+            within(u, LAG2_PAIR, paired, 1)
+            within(u, LAG2_TOTAL, totalled, 1)
+
+        when(u == done + 9, w_along_z)
+        s = u - LAG2_SHARE - 1
+
+        @pl.when((s >= 0) & (s % 2 == 0))
+        def _():
+            proj_some([s, s + 1])
+            when(s >= 2, final, [s - 2, s - 1])
+
+        return carry
+
+    lax.fori_loop(0, LAG_MLP, fill, 0)
+    lax.fori_loop(0, pairs + 1, middle_two, 0)
+    lax.fori_loop(samples + LAG_MLP + 1, samples - 2 + LAG2_SHARE, drain, 0)
     last = [samples - 2, samples - 1]
-    proj = (proj_acc[...] + proj_of(last)).reshape(32, 8, 256)
-    proj = jnp.concatenate([proj[..., :128], proj[..., 128:]], axis=1)
-    p_mine[...] = proj.astype(BF)
-    p_copies = []
-    for d in range(1, 32):
-        there = (dp + d) % 32
-        p_copies.append(send(p_mine.at[there], p_land.at[d], pss, prs, (there, ft)))
-    for copy in p_copies:
-        copy.start()
-    p_all = send(p_mine.at[pl.ds(0, 31)], p_land.at[pl.ds(1, 31)], pss, prs, buddy)
+
+    @pl.when(outer)
+    def _():
+        for s in last:
+            shared(1, s)
+
+    here = p_land.at[pl.ds(dp, 1)]
+    for i in range(2):
+        proj = (proj_acc[i] + proj_of(i == 0, last)).reshape(16, 8, 256)
+        p_mine[i] = jnp.concatenate([proj[..., :128], proj[..., 128:]], axis=1).astype(BF)
+    for dh, dy, xi, i in itertools.product((1, 0), (2, 1, 3, 0), (0, 1), (0, 1)):
+        there = xi * 8 + ((y + dy) % 4) * 2 + (hi + dh) % 2
+        core = c if i == 0 else 1 - c
+        copy = send(p_mine.at[i, pl.ds(there, 1)], here, pss, prs, (half * 16 + there, z * 2 + core))
+        if dh == 0 and dy == 0 and i == 0:
+            pl.when(half * 2 + xi != x)(copy.start)
+        else:
+            copy.start()
+
+    @pl.when(hi_half == half)
+    def _():
+        p_land[dp] = p_mine[0, dp % 16]
+
+    def p_some(count):
+        return send(p_land.at[pl.ds(0, count)], p_land.at[pl.ds(0, count)], pss, prs, buddy)
+
+    final([samples - 4, samples - 3])
+    for s in last:
+        share(1, s).wait_recv()
     grad_of(last)
     w_share()
 
@@ -361,13 +433,16 @@
     hg_ref[:, 256:] = w_all[8:, :256] * mlp_scale
     og_ref[...] = w_all[:, 256:] * mlp_scale
     pltpu.make_async_copy(stage, eg_any, store_sem).wait()
-    p_all.wait_recv()
-    total = p_mine[dp].astype(F32)
+    pl.when(hi_half == half)(lambda: p_some(31).wait_recv())
+    pl.when(hi_half != half)(lambda: p_some(32).wait_recv())
+    total = p_land[0].astype(F32)
     for d in range(1, 32):
         total += p_land[d].astype(F32)
     pg_ref[:, :128] = total[:8] * proj_scale
     pg_ref[:, 128:] = total[8:] * proj_scale
-    p_all.wait_send()
+    swap.wait_send()
+    pl.when(hi_half == half)(lambda: p_some(31).wait_send())
+    pl.when(hi_half != half)(lambda: p_some(32).wait_send())
 
 
 def finish(eg_in, pg_in, hg_in, og_in, eg_out, pg_out, hg_out, og_out, eg, pg, hg, og, in_sem, out_sem):
@@ -421,17 +496,19 @@
             vmem((2, n, k // 2, d), BF),
             vmem((2, n, k // 2, d), BF),
             vmem((2, n, k, d), BF),
-            vmem((n, f, d), F32),
+            vmem((n, h, f), F32),
+            vmem((n, k, f), BF),
+            [vmem((k, f), BF)] * 2, [vmem((h, f), BF)] * 2, [vmem((h, f), BF)] * 2,
             vmem((n, f, d), BF),
-            vmem((k, h), F32), vmem((h, d), F32), vmem((k, f), F32),
+            vmem((k, h), F32), vmem((h, d), F32), vmem((2, k // 2, f), F32),
             vmem((16, 2, 16, 384), BF), vmem((16, 16, 384), BF), vmem((16, 16, 384), BF),
             vmem((16, 16, 384), BF), vmem((16, 384), BF), vmem((8, 16, 384), BF), vmem((16, 384), F32),
-            vmem((32, 16, 128), BF), vmem((32, 16, 128), BF),
-            dma((5,)), dma, dma((2, 4)), dma((2, n, 4)),
-            dma((4,)), dma((4,)), dma, dma, pltpu.SemaphoreType.REGULAR((5,)),
+            vmem((2, 16, 16, 128), BF), vmem((32, 16, 128), BF), vmem((n, f, d), BF),
+            dma((5,)), dma, dma((2, 5)), dma((2, n, 5)),
+            dma((4,)), dma((4,)), dma, dma, pltpu.SemaphoreType.REGULAR((4,)),
         ],
         compiler_params=pltpu.CompilerParams(
-            collective_id=0, has_side_effects=True, vmem_limit_bytes=60 * 1024 * 1024
+            collective_id=0, has_side_effects=True, vmem_limit_bytes=int(53.9 * 1024) * 1024
         ),
     )(embeds, proj_weight, hidden_weight, out_weight, cotangent)
     grad, proj, hid, out = pl.pallas_call(
@@ -440,7 +517,7 @@
         in_specs=[hbm] * 4,
         out_specs=(hbm,) * 4,
         scratch_shapes=[vmem(v.shape, v.dtype) for v in shapes] + [dma((7,)), dma((7,))],
-        compiler_params=pltpu.CompilerParams(vmem_limit_bytes=60 * 1024 * 1024),
+        compiler_params=pltpu.CompilerParams(vmem_limit_bytes=int(53.9 * 1024) * 1024),
     )(*results)
     return grad, proj.T, hid, out
 

time: 59.6 us -> 57.9 us (0.971)
  Pallas kernels: 58.8 us -> 57.1 us
    pallas_call x1, Pallas kernels: 56.8 us -> 55 us  [local(): pl.pallas_call(functools.partial(kernel, n, proj_scale, mlp_scale), out_s...]
where the time goes in v4:
time: 57.9 us; the launch traced here: 57.7 us
  Pallas kernels  57.1 us (99%)
  between operations  0.64 us (1%)
    pallas_call x1, Pallas kernels, local(): pl.pallas_call(functools.partial(kernel, n, proj_scale, mlp_scale), out_s...  55 us
    pallas_call x1, Pallas kernels, local(): pl.pallas_call(finish, out_shape=shapes, in_specs=[hbm] * 4, out_specs=(h...  2.09 us

profile of v4, /device:TPU:1, one launch (start us, length us, event | category | flops | bytes accessed | tf_op | source)
XLA Modules:
  0.0 57.7 jit_solution(17226124252943325176)
XLA Ops:
  0.6 55.0 %shard_map.84 = (bf16[16,256,128]{2,1,0:T(8,128)(2,1)}, f32[8,256]{1,0:T(8,128)S(1)}, f32[8,512]{1,0:T(8,128)S(1)}, f32[16,128]{1,0:T(8,128)S(1)}) custom-call(bf16[16,256,128]{2,1,0:T(8,128)(2,1)} %e_hbm.1, bf16[256,256]{1,0:T(8,128)(2,1)} %p_hbm.1, bf16[256,512]{1,0:T(8,128)(2,1)} %w1_hbm.1, bf16[512,128]{1,0:T(8,128)(2,1)} %w2_hbm.1, ...), custom_call_target="tpu_custom_call" | custom-call | tf_op jit(solution)/shard_map/pallas_call | solution.py:484
  55.6 2.1 %shard_map.85 = (bf16[16,256,128]{2,1,0:T(8,128)(2,1)}, f32[8,256]{1,0:T(8,128)}, f32[8,512]{1,0:T(8,128)}, f32[16,128]{1,0:T(8,128)}) custom-call(bf16[16,256,128]{2,1,0:T(8,128)(2,1)} %get-tuple-element.12.eg_in, f32[8,256]{1,0:T(8,128)S(1)} %get-tuple-element.13.pg_in, f32[8,512]{1,0:T(8,128)S(1)} %get-tuple-element.14.hg_in, ...), custom_call_target="tpu_custom_call" | custom-call | tf_op jit(solution)/shard_map/pallas_call | solution.py:514

commit v5 on v4

--- a/solution.py
+++ b/solution.py
@@ -16,10 +16,10 @@
 LAG_TOTAL = 5
 LAG_SHARE = 10
 LAG_MLP = 12
-LAG2_FIRST = 15
-LAG2_PAIR = 20
-LAG2_TOTAL = 25
-LAG2_SHARE = 30
+LAG2_FIRST = 14
+LAG2_PAIR = 19
+LAG2_TOTAL = 24
+LAG2_SHARE = 29
 
 
 def nn(a, b):
@@ -36,13 +36,13 @@
 
 def kernel(
     samples, proj_scale, mlp_scale, e_hbm, p_hbm, w1_hbm, w2_hbm, c_hbm,
-    eg_any, pg_ref, hg_ref, og_ref,
+    eg_ref, pg_ref, hg_ref, og_ref,
     e_ref, p_ref, w1_ref, w2_ref, c_ref, pt_ref, w1t_ref, w2h_ref,
     part, land_a, chip, land_b, pair, land_c, full,
-    act_cot, icot, inters, acts, pre_cots, stage, hid_acc, out_acc, proj_acc,
+    act_cot, icot, inters, acts, pre_cots, hid_acc, out_acc, proj_acc,
     w_mine, w_buddy, w_chip, w_xy, w_plane, w_z, w_all,
     p_mine, p_land,
-    e2_ref, load_sem, store_sem, ssem, rsem, wss, wrs, pss, prs, relay,
+    e2_ref, load_sem, ssem, rsem, wss, wrs, pss, prs, relay,
 ):
     pairs = samples // 2
     dp, ft = lax.axis_index("dp"), lax.axis_index("feat")
@@ -178,7 +178,7 @@
     hid_acc[...] = jnp.zeros_like(hid_acc)
     out_acc[...] = jnp.zeros_like(out_acc)
     proj_acc[...] = jnp.zeros_like(proj_acc)
-    for ref in (*inters, *acts, *pre_cots):
+    for ref in (inters, acts, pre_cots):
         ref[...] = jnp.zeros_like(ref)
     for load in loads[2:]:
         load.wait()
@@ -203,25 +203,24 @@
     def mlp(s, now, before):
         r = jnp.maximum(s - 1, 0)
         s = jnp.minimum(s, samples - 1)
-        inter_cot = nn(w1_ref[...], pre_cots[before][...]).astype(BF)
+        inter_cot = nn(w1_ref[...], pre_cots[before]).astype(BF)
         icot[r] = inter_cot
         inter = nt(full[0, s], e_ref[s]).astype(BF)
-        hid_acc[...] += nt(inters[before][...], pre_cots[before][...])
+        hid_acc[...] += nt(inters[before], pre_cots[before])
         u = nn(w1t_ref[...], inter)
-        out_acc[...] += nn(acts[before][...], c_ref[r])
+        out_acc[...] += nn(acts[before], c_ref[r])
         t = jnp.tanh(u)
         p = 1.0 + t
         a = u * p
-        inters[now][...] = inter
-        acts[now][...] = a.astype(BF)
-        pre_cots[now][...] = (act_cot[s] * (p + a * (1.0 - t))).astype(BF)
+        inters[now] = inter
+        acts[now] = a.astype(BF)
+        pre_cots[now] = (act_cot[s] * (p + a * (1.0 - t))).astype(BF)
         part[1, r] = nn(inter_cot, e_ref[r]).astype(BF)
 
     def grad_of(both):
         for s in both:
             total = tn(icot[s], full[0, s]) + nn(p_ref[...], full[1, s])
-            stage[s] = (c_ref[s].astype(F32) + total).astype(BF)
-            pltpu.make_async_copy(stage.at[s], eg_any.at[s], store_sem).start()
+            eg_ref[s] = (c_ref[s].astype(F32) + total).astype(BF)
 
     def proj_of(own, both):
         emb = e_ref if own else e2_ref
@@ -312,8 +311,9 @@
         when(outer & (u >= LAG_SHARE), shared, 0, u - LAG_SHARE)
         return carry
 
-    def middle(s, now):
+    def middle(s, carry):
         u = s + LAG_MLP
+        now = s % 2
 
         @pl.when(hub)
         def _():
@@ -340,9 +340,6 @@
             within(u, LAG2_PAIR, paired, 1)
             within(u, LAG2_TOTAL, totalled, 1)
 
-    def middle_two(i, carry):
-        middle(2 * i, 0)
-        when(i < pairs, middle, 2 * i + 1, 1)
         return carry
 
     def drain(u, carry):
@@ -373,7 +370,7 @@
         return carry
 
     lax.fori_loop(0, LAG_MLP, fill, 0)
-    lax.fori_loop(0, pairs + 1, middle_two, 0)
+    lax.fori_loop(0, samples + 1, middle, 0)
     lax.fori_loop(samples + LAG_MLP + 1, samples - 2 + LAG2_SHARE, drain, 0)
     last = [samples - 2, samples - 1]
 
@@ -432,7 +429,6 @@
     hg_ref[:, :256] = w_all[:8, :256] * mlp_scale
     hg_ref[:, 256:] = w_all[8:, :256] * mlp_scale
     og_ref[...] = w_all[:, 256:] * mlp_scale
-    pltpu.make_async_copy(stage, eg_any, store_sem).wait()
     pl.when(hi_half == half)(lambda: p_some(31).wait_recv())
     pl.when(hi_half != half)(lambda: p_some(32).wait_recv())
     total = p_land[0].astype(F32)
@@ -445,22 +441,13 @@
     pl.when(hi_half != half)(lambda: p_some(32).wait_send())
 
 
-def finish(eg_in, pg_in, hg_in, og_in, eg_out, pg_out, hg_out, og_out, eg, pg, hg, og, in_sem, out_sem):
-    parts = in_sem.shape[0] - 3
-    rows = eg.shape[0] // parts
-    moves = [(pg_in, pg, pg_out), (hg_in, hg, hg_out), (og_in, og, og_out)]
-    for i in range(parts):
-        some = pl.ds(i * rows, rows)
-        moves.append((eg_in.at[some], eg.at[some], eg_out.at[some]))
-    loads = [pltpu.make_async_copy(m[0], m[1], in_sem.at[i]) for i, m in enumerate(moves)]
-    stores = [pltpu.make_async_copy(m[1], m[2], out_sem.at[i]) for i, m in enumerate(moves)]
-    for load in loads:
-        load.start()
-    for load, store in zip(loads, stores):
-        load.wait()
-        store.start()
-    for store in stores:
-        store.wait()
+def finish(*refs):
+    count = (len(refs) - 1) // 2
+    copies = [pltpu.make_async_copy(refs[i], refs[count + i], refs[-1].at[i]) for i in range(count)]
+    for copy in copies:
+        copy.start()
+    for copy in copies:
+        copy.wait()
 
 
 def local(embeds, proj_weight, hidden_weight, out_weight, cotangent):
@@ -483,9 +470,9 @@
     )
     results = pl.pallas_call(
         functools.partial(kernel, n, proj_scale, mlp_scale),
-        out_shape=shapes,
+        out_shape=tuple(vmem(v.shape, v.dtype) for v in shapes),
         in_specs=[hbm] * 5,
-        out_specs=(anywhere, inside, inside, inside),
+        out_specs=(inside,) * 4,
         scratch_shapes=[
             vmem((n, f, d), BF), vmem((f, k), BF), vmem((k, h), BF), vmem((h, d), BF), vmem((n, f, d), BF),
             vmem((k, f), BF), vmem((h, k), BF), vmem((h, d), BF),
@@ -498,26 +485,25 @@
             vmem((2, n, k, d), BF),
             vmem((n, h, f), F32),
             vmem((n, k, f), BF),
-            [vmem((k, f), BF)] * 2, [vmem((h, f), BF)] * 2, [vmem((h, f), BF)] * 2,
-            vmem((n, f, d), BF),
+            vmem((2, k, f), BF), vmem((2, h, f), BF), vmem((2, h, f), BF),
             vmem((k, h), F32), vmem((h, d), F32), vmem((2, k // 2, f), F32),
             vmem((16, 2, 16, 384), BF), vmem((16, 16, 384), BF), vmem((16, 16, 384), BF),
             vmem((16, 16, 384), BF), vmem((16, 384), BF), vmem((8, 16, 384), BF), vmem((16, 384), F32),
             vmem((2, 16, 16, 128), BF), vmem((32, 16, 128), BF), vmem((n, f, d), BF),
-            dma((5,)), dma, dma((2, 5)), dma((2, n, 5)),
+            dma((5,)), dma((2, 5)), dma((2, n, 5)),
             dma((4,)), dma((4,)), dma, dma, pltpu.SemaphoreType.REGULAR((4,)),
         ],
         compiler_params=pltpu.CompilerParams(
-            collective_id=0, has_side_effects=True, vmem_limit_bytes=int(53.9 * 1024) * 1024
+            collective_id=0, has_side_effects=True, vmem_limit_bytes=48 * 1024 * 1024
         ),
-    )(embeds, proj_weight, hidden_weight, out_weight, cotangent)
+    )(*[pltpu.with_memory_space_constraint(v, pltpu.HBM) for v in (embeds, proj_weight, hidden_weight, out_weight, cotangent)])
     grad, proj, hid, out = pl.pallas_call(
         finish,
         out_shape=shapes,
-        in_specs=[hbm] * 4,
+        in_specs=[inside] * 4,
         out_specs=(hbm,) * 4,
-        scratch_shapes=[vmem(v.shape, v.dtype) for v in shapes] + [dma((7,)), dma((7,))],
-        compiler_params=pltpu.CompilerParams(vmem_limit_bytes=int(53.9 * 1024) * 1024),
+        scratch_shapes=[dma((4,))],
+        compiler_params=pltpu.CompilerParams(vmem_limit_bytes=48 * 1024 * 1024),
     )(*results)
     return grad, proj.T, hid, out
 

time: 57.9 us -> 56.5 us (0.976)
  Pallas kernels: 57.1 us -> 55.8 us
    pallas_call x1, Pallas kernels: 2.09 us -> 1.01 us  [local(): pl.pallas_call(finish, out_shape=shapes, in_specs=[inside] * 4, out_specs...]
where the time goes in v5:
time: 56.5 us; the launch traced here: 56.4 us
  Pallas kernels  55.8 us (99%)
  between operations  0.64 us (1%)
    pallas_call x1, Pallas kernels, local(): pl.pallas_call(functools.partial(kernel, n, proj_scale, mlp_scale), out_s...  54.8 us

profile of v5, /device:TPU:1, one launch (start us, length us, event | category | flops | bytes accessed | tf_op | source)
XLA Modules:
  0.0 56.4 jit_solution(2653192167722745536)
XLA Ops:
  0.6 54.8 %shard_map.84 = (bf16[16,256,128]{2,1,0:T(8,128)(2,1)S(1)}, f32[8,256]{1,0:T(8,128)S(1)}, f32[8,512]{1,0:T(8,128)S(1)}, f32[16,128]{1,0:T(8,128)S(1)}) custom-call(bf16[16,256,128]{2,1,0:T(8,128)(2,1)} %e_hbm.1, bf16[256,256]{1,0:T(8,128)(2,1)} %p_hbm.1, bf16[256,512]{1,0:T(8,128)(2,1)} %w1_hbm.1, bf16[512,128]{1,0:T(8,128)(2,1)} %w2_hbm.1, ...), custom_call_target="tpu_custom_call" | custom-call | tf_op jit(solution)/shard_map/pallas_call | solution.py:471
  55.4 1.0 %shard_map.85 = (bf16[16,256,128]{2,1,0:T(8,128)(2,1)}, f32[8,256]{1,0:T(8,128)}, f32[8,512]{1,0:T(8,128)}, f32[16,128]{1,0:T(8,128)}) custom-call(bf16[16,256,128]{2,1,0:T(8,128)(2,1)S(1)} %get-tuple-element.12.refs_0_, f32[8,256]{1,0:T(8,128)S(1)} %get-tuple-element.13.refs_1_, f32[8,512]{1,0:T(8,128)S(1)} %get-tuple-element.14.refs_2_, ...), custom_call_target="tpu_custom_call" | custom-call | tf_op jit(solution)/shard_map/pallas_call | solution.py:500

commit v6 on v5

--- a/solution.py
+++ b/solution.py
@@ -13,13 +13,14 @@
 BF = jnp.bfloat16
 F32 = jnp.float32
 
-LAG_TOTAL = 5
-LAG_SHARE = 10
-LAG_MLP = 12
-LAG2_FIRST = 14
-LAG2_PAIR = 19
-LAG2_TOTAL = 24
-LAG2_SHARE = 29
+LAG_TOTAL = 4
+LAG_SHARE = 8
+LAG_MLP = 10
+LAG_MLP_HUB = 6
+LAG2_FIRST = 12
+LAG2_PAIR = 17
+LAG2_TOTAL = 21
+LAG2_SHARE = 27
 
 
 def nn(a, b):
@@ -299,12 +300,13 @@
     def within(u, lag, act, *args):
         when((u >= lag) & (u < lag + samples), act, *args, u - lag)
 
+    lag_mlp = jnp.where(hub, LAG_MLP_HUB, LAG_MLP)
+
     def fill(u, carry):
         @pl.when(hub)
         def _():
             when(u == 0, hear, 0)
             when(u == 0, tell, 1)
-            when(u == 8, hear, 1)
             paired(0, u)
             when(u >= LAG_TOTAL, totalled, 0, u - LAG_TOTAL)
 
@@ -312,11 +314,12 @@
         return carry
 
     def middle(s, carry):
-        u = s + LAG_MLP
+        u = s + lag_mlp
         now = s % 2
 
         @pl.when(hub)
         def _():
+            when(u == 8, hear, 1)
             within(u, 0, paired, 0)
             within(u, LAG_TOTAL, totalled, 0)
 
@@ -343,22 +346,22 @@
         return carry
 
     def drain(u, carry):
-        done = samples + LAG_MLP + 1
+        done = samples + lag_mlp + 1
+
+        @pl.when(outer)
+        def _():
+            when(u == LAG2_FIRST + samples - 1, hear_ring, 3)
+            within(u, LAG2_FIRST, first, 1)
+            when(u >= LAG2_SHARE, shared, 1, u - LAG2_SHARE)
+
+        @pl.when(hub)
+        def _():
+            within(u, LAG2_PAIR, paired, 1)
+            within(u, LAG2_TOTAL, totalled, 1)
+
         when(u == done, w_first)
         when(u == done, swap.wait_recv)
         when(u == done + 2, w_along_xy)
-
-        @pl.when(outer)
-        def _():
-            when(u == LAG2_FIRST + samples - 1, hear_ring, 3)
-            within(u, LAG2_FIRST, first, 1)
-            when(u >= LAG2_SHARE, shared, 1, u - LAG2_SHARE)
-
-        @pl.when(hub)
-        def _():
-            within(u, LAG2_PAIR, paired, 1)
-            within(u, LAG2_TOTAL, totalled, 1)
-
         when(u == done + 9, w_along_z)
         s = u - LAG2_SHARE - 1
 
@@ -369,19 +372,24 @@
 
         return carry
 
-    lax.fori_loop(0, LAG_MLP, fill, 0)
+    lax.fori_loop(0, lag_mlp, fill, 0)
     lax.fori_loop(0, samples + 1, middle, 0)
-    lax.fori_loop(samples + LAG_MLP + 1, samples - 2 + LAG2_SHARE, drain, 0)
+    lax.fori_loop(samples + lag_mlp + 1, samples - 2 + LAG2_SHARE, drain, 0)
     last = [samples - 2, samples - 1]
 
     @pl.when(outer)
     def _():
-        for s in last:
-            shared(1, s)
+        shared(1, samples - 2)
+
+    proj_some([samples - 2])
+
+    @pl.when(outer)
+    def _():
+        shared(1, samples - 1)
 
     here = p_land.at[pl.ds(dp, 1)]
     for i in range(2):
-        proj = (proj_acc[i] + proj_of(i == 0, last)).reshape(16, 8, 256)
+        proj = (proj_acc[i] + proj_of(i == 0, [samples - 1])).reshape(16, 8, 256)
         p_mine[i] = jnp.concatenate([proj[..., :128], proj[..., 128:]], axis=1).astype(BF)
     for dh, dy, xi, i in itertools.product((1, 0), (2, 1, 3, 0), (0, 1), (0, 1)):
         there = xi * 8 + ((y + dy) % 4) * 2 + (hi + dh) % 2

time: 56.5 us -> 55.4 us (0.981)
  Pallas kernels: 55.8 us -> 54.7 us
    pallas_call x1, Pallas kernels: 54.8 us -> 53.7 us  [local(): pl.pallas_call(functools.partial(kernel, n, proj_scale, mlp_scale), out_s...]
where the time goes in v6:
time: 55.4 us; the launch traced here: 55.3 us
  Pallas kernels  54.7 us (99%)
  between operations  0.64 us (1%)
    pallas_call x1, Pallas kernels, local(): pl.pallas_call(functools.partial(kernel, n, proj_scale, mlp_scale), out_s...  53.7 us

profile of v6, /device:TPU:1, one launch (start us, length us, event | category | flops | bytes accessed | tf_op | source)
XLA Modules:
  0.0 55.3 jit_solution(1339543247473690426)
XLA Ops:
  0.6 53.7 %shard_map.84 = (bf16[16,256,128]{2,1,0:T(8,128)(2,1)S(1)}, f32[8,256]{1,0:T(8,128)S(1)}, f32[8,512]{1,0:T(8,128)S(1)}, f32[16,128]{1,0:T(8,128)S(1)}) custom-call(bf16[16,256,128]{2,1,0:T(8,128)(2,1)} %e_hbm.1, bf16[256,256]{1,0:T(8,128)(2,1)} %p_hbm.1, bf16[256,512]{1,0:T(8,128)(2,1)} %w1_hbm.1, bf16[512,128]{1,0:T(8,128)(2,1)} %w2_hbm.1, ...), custom_call_target="tpu_custom_call" | custom-call | tf_op jit(solution)/shard_map/pallas_call | solution.py:479
  54.3 1.0 %shard_map.85 = (bf16[16,256,128]{2,1,0:T(8,128)(2,1)}, f32[8,256]{1,0:T(8,128)}, f32[8,512]{1,0:T(8,128)}, f32[16,128]{1,0:T(8,128)}) custom-call(bf16[16,256,128]{2,1,0:T(8,128)(2,1)S(1)} %get-tuple-element.12.refs_0_, f32[8,256]{1,0:T(8,128)S(1)} %get-tuple-element.13.refs_1_, f32[8,512]{1,0:T(8,128)S(1)} %get-tuple-element.14.refs_2_, ...), custom_call_target="tpu_custom_call" | custom-call | tf_op jit(solution)/shard_map/pallas_call | solution.py:508

commit v7 on v6

--- a/solution.py
+++ b/solution.py
@@ -18,8 +18,8 @@
 LAG_MLP = 10
 LAG_MLP_HUB = 6
 LAG2_FIRST = 12
-LAG2_PAIR = 17
-LAG2_TOTAL = 21
+LAG2_PAIR = 16
+LAG2_TOTAL = 20
 LAG2_SHARE = 27
 
 
@@ -323,16 +323,13 @@
             within(u, 0, paired, 0)
             within(u, LAG_TOTAL, totalled, 0)
 
-        @pl.when(outer)
-        def _():
-            within(u, LAG_SHARE, shared, 0)
-
         when(s < samples, lambda: share(0, s).wait_recv())
         mlp(s, now, 1 - now)
         when(s > 0, lambda: to_buddy(1, s - 1).start())
 
         @pl.when(outer)
         def _():
+            within(u, LAG_SHARE, shared, 0)
             when(s == 0, tell_ring, 2)
             when(s == 8, hear_ring, 2)
             when(s == 13, tell_ring, 3)
@@ -361,21 +358,19 @@
 
         when(u == done, w_first)
         when(u == done, swap.wait_recv)
-        when(u == done + 2, w_along_xy)
-        when(u == done + 9, w_along_z)
+        when(u == done + 3, w_along_xy)
+        when(u == done + 10, w_along_z)
         s = u - LAG2_SHARE - 1
 
         @pl.when((s >= 0) & (s % 2 == 0))
         def _():
             proj_some([s, s + 1])
-            when(s >= 2, final, [s - 2, s - 1])
 
         return carry
 
     lax.fori_loop(0, lag_mlp, fill, 0)
     lax.fori_loop(0, samples + 1, middle, 0)
     lax.fori_loop(samples + lag_mlp + 1, samples - 2 + LAG2_SHARE, drain, 0)
-    last = [samples - 2, samples - 1]
 
     @pl.when(outer)
     def _():
@@ -407,11 +402,13 @@
     def p_some(count):
         return send(p_land.at[pl.ds(0, count)], p_land.at[pl.ds(0, count)], pss, prs, buddy)
 
-    final([samples - 4, samples - 3])
-    for s in last:
-        share(1, s).wait_recv()
-    grad_of(last)
+    def finals(i, carry):
+        final([2 * i, 2 * i + 1])
+        return carry
+
+    lax.fori_loop(0, pairs // 2, finals, 0)
     w_share()
+    lax.fori_loop(pairs // 2, pairs, finals, 0)
 
     for q in range(2):
         sent = [send(chip.at[q], land_b.at[q], ssem.at[q, k], rsem.at[q, 0, 0], buddy) for k in range(4)]

time: 55.4 us -> 54.7 us (0.987)
  Pallas kernels: 54.7 us -> 53.9 us
    pallas_call x1, Pallas kernels: 53.7 us -> 52.9 us  [local(): pl.pallas_call(functools.partial(kernel, n, proj_scale, mlp_scale), out_s...]
where the time goes in v7:
time: 54.7 us; the launch traced here: 54.6 us
  Pallas kernels  53.9 us (99%)
  between operations  0.64 us (1%)
    pallas_call x1, Pallas kernels, local(): pl.pallas_call(functools.partial(kernel, n, proj_scale, mlp_scale), out_s...  52.9 us

profile of v7, /device:TPU:1, one launch (start us, length us, event | category | flops | bytes accessed | tf_op | source)
XLA Modules:
  0.0 54.6 jit_solution(13811267619733761877)
XLA Ops:
  0.6 52.9 %shard_map.84 = (bf16[16,256,128]{2,1,0:T(8,128)(2,1)S(1)}, f32[8,256]{1,0:T(8,128)S(1)}, f32[8,512]{1,0:T(8,128)S(1)}, f32[16,128]{1,0:T(8,128)S(1)}) custom-call(bf16[16,256,128]{2,1,0:T(8,128)(2,1)} %e_hbm.1, bf16[256,256]{1,0:T(8,128)(2,1)} %p_hbm.1, bf16[256,512]{1,0:T(8,128)(2,1)} %w1_hbm.1, bf16[512,128]{1,0:T(8,128)(2,1)} %w2_hbm.1, ...), custom_call_target="tpu_custom_call" | custom-call | tf_op jit(solution)/shard_map/pallas_call | solution.py:476
  53.6 1.0 %shard_map.85 = (bf16[16,256,128]{2,1,0:T(8,128)(2,1)}, f32[8,256]{1,0:T(8,128)}, f32[8,512]{1,0:T(8,128)}, f32[16,128]{1,0:T(8,128)}) custom-call(bf16[16,256,128]{2,1,0:T(8,128)(2,1)S(1)} %get-tuple-element.12.refs_0_, f32[8,256]{1,0:T(8,128)S(1)} %get-tuple-element.13.refs_1_, f32[8,512]{1,0:T(8,128)S(1)} %get-tuple-element.14.refs_2_, ...), custom_call_target="tpu_custom_call" | custom-call | tf_op jit(solution)/shard_map/pallas_call | solution.py:505

commit v8 on v7

--- a/solution.py
+++ b/solution.py
@@ -71,7 +71,7 @@
     opposite = [(((x + 2) % 4) * 8 + y * 2 + hi, ft), (x * 8 + ((y + 2) % 4) * 2 + hi, ft)]
 
     barrier = pltpu.get_barrier_semaphore()
-    peers = [buddy, edge, third] + sides
+    peers = sides + [edge, third, buddy]
     for peer in peers:
         pl.semaphore_signal(barrier, inc=1, device_id=peer, device_id_type=MESH)
 
@@ -332,7 +332,7 @@
             within(u, LAG_SHARE, shared, 0)
             when(s == 0, tell_ring, 2)
             when(s == 8, hear_ring, 2)
-            when(s == 13, tell_ring, 3)
+            when(s == 12, tell_ring, 3)
             within(u, LAG2_FIRST, first, 1)
 
         @pl.when(hub)
@@ -447,8 +447,12 @@
 
 
 def finish(*refs):
+    sem = refs[-1]
     count = (len(refs) - 1) // 2
-    copies = [pltpu.make_async_copy(refs[i], refs[count + i], refs[-1].at[i]) for i in range(count)]
+    rows = refs[0].shape[0] // 4
+    pairs = [(refs[0].at[pl.ds(i * rows, rows)], refs[count].at[pl.ds(i * rows, rows)]) for i in range(4)]
+    pairs += [(refs[i], refs[count + i]) for i in range(1, count)]
+    copies = [pltpu.make_async_copy(src, dst, sem.at[i]) for i, (src, dst) in enumerate(pairs)]
     for copy in copies:
         copy.start()
     for copy in copies:
@@ -507,7 +511,7 @@
         out_shape=shapes,
         in_specs=[inside] * 4,
         out_specs=(hbm,) * 4,
-        scratch_shapes=[dma((4,))],
+        scratch_shapes=[dma((7,))],
         compiler_params=pltpu.CompilerParams(vmem_limit_bytes=48 * 1024 * 1024),
     )(*results)
     return grad, proj.T, hid, out

time: 54.7 us -> 54.8 us (level)
  no operation moved by 1% of the time
where the time goes in v8:
time: 54.8 us; the launch traced here: 54.7 us
  Pallas kernels  54 us (99%)
  between operations  0.64 us (1%)
    pallas_call x1, Pallas kernels, local(): pl.pallas_call(functools.partial(kernel, n, proj_scale, mlp_scale), out_s...  53 us

profile of v8, /device:TPU:1, one launch (start us, length us, event | category | flops | bytes accessed | tf_op | source)
XLA Modules:
  0.0 54.7 jit_solution(603095596927805714)
XLA Ops:
  0.6 53.0 %shard_map.84 = (bf16[16,256,128]{2,1,0:T(8,128)(2,1)S(1)}, f32[8,256]{1,0:T(8,128)S(1)}, f32[8,512]{1,0:T(8,128)S(1)}, f32[16,128]{1,0:T(8,128)S(1)}) custom-call(bf16[16,256,128]{2,1,0:T(8,128)(2,1)} %e_hbm.1, bf16[256,256]{1,0:T(8,128)(2,1)} %p_hbm.1, bf16[256,512]{1,0:T(8,128)(2,1)} %w1_hbm.1, bf16[512,128]{1,0:T(8,128)(2,1)} %w2_hbm.1, ...), custom_call_target="tpu_custom_call" | custom-call | tf_op jit(solution)/shard_map/pallas_call | solution.py:480
  53.6 1.0 %shard_map.85 = (bf16[16,256,128]{2,1,0:T(8,128)(2,1)}, f32[8,256]{1,0:T(8,128)}, f32[8,512]{1,0:T(8,128)}, f32[16,128]{1,0:T(8,128)}) custom-call(bf16[16,256,128]{2,1,0:T(8,128)(2,1)S(1)} %get-tuple-element.12.refs_0_, f32[8,256]{1,0:T(8,128)S(1)} %get-tuple-element.13.refs_1_, f32[8,512]{1,0:T(8,128)S(1)} %get-tuple-element.14.refs_2_, ...), custom_call_target="tpu_custom_call" | custom-call | tf_op jit(solution)/shard_map/pallas_call | solution.py:509

commit v9 on v7

--- a/solution.py
+++ b/solution.py
@@ -18,8 +18,8 @@
 LAG_MLP = 10
 LAG_MLP_HUB = 6
 LAG2_FIRST = 12
-LAG2_PAIR = 16
-LAG2_TOTAL = 20
+LAG2_PAIR = 15
+LAG2_TOTAL = 19
 LAG2_SHARE = 27
 
 

time: 54.7 us -> 54.8 us (level)
  no operation moved by 1% of the time
where the time goes in v9:
time: 54.8 us; the launch traced here: 54.7 us
  Pallas kernels  54.1 us (99%)
  between operations  0.64 us (1%)
    pallas_call x1, Pallas kernels, local(): pl.pallas_call(functools.partial(kernel, n, proj_scale, mlp_scale), out_s...  53.1 us

profile of v9, /device:TPU:1, one launch (start us, length us, event | category | flops | bytes accessed | tf_op | source)
XLA Modules:
  0.0 54.7 jit_solution(1757348852776219767)
XLA Ops:
  0.6 53.1 %shard_map.84 = (bf16[16,256,128]{2,1,0:T(8,128)(2,1)S(1)}, f32[8,256]{1,0:T(8,128)S(1)}, f32[8,512]{1,0:T(8,128)S(1)}, f32[16,128]{1,0:T(8,128)S(1)}) custom-call(bf16[16,256,128]{2,1,0:T(8,128)(2,1)} %e_hbm.1, bf16[256,256]{1,0:T(8,128)(2,1)} %p_hbm.1, bf16[256,512]{1,0:T(8,128)(2,1)} %w1_hbm.1, bf16[512,128]{1,0:T(8,128)(2,1)} %w2_hbm.1, ...), custom_call_target="tpu_custom_call" | custom-call | tf_op jit(solution)/shard_map/pallas_call | solution.py:476
  53.7 1.0 %shard_map.85 = (bf16[16,256,128]{2,1,0:T(8,128)(2,1)}, f32[8,256]{1,0:T(8,128)}, f32[8,512]{1,0:T(8,128)}, f32[16,128]{1,0:T(8,128)}) custom-call(bf16[16,256,128]{2,1,0:T(8,128)(2,1)S(1)} %get-tuple-element.12.refs_0_, f32[8,256]{1,0:T(8,128)S(1)} %get-tuple-element.13.refs_1_, f32[8,512]{1,0:T(8,128)S(1)} %get-tuple-element.14.refs_2_, ...), custom_call_target="tpu_custom_call" | custom-call | tf_op jit(solution)/shard_map/pallas_call | solution.py:505
